TPU v7x, 32 devices: a whole 2x2x4 slice. The times are simulated.
32 devices in a mesh: dp: 8 (over y, x, core), feat: 4 (over z).
Axes of the slice: x: 2, y: 2, z: 4, core: 2. Of those that a mesh axis runs over, the one named last changes fastest.
Arguments:
- tokens: bfloat16 [4096, 16384], P('dp', 'feat'), may hold values from -6 to 6
- weight: bfloat16 [32, 6, 512, 512], P('feat'), may hold values from -0.15625 to 0.15625
- cotangent: bfloat16 [4096, 16384], P('dp', 'feat'), may hold values from -6 to 6
Outputs:
- output: bfloat16 [4096, 16384], P('dp', 'feat')
- input_grad: bfloat16 [4096, 16384], P('dp', 'feat')
- weight_grad: float32 [32, 6, 512, 512], P('feat', None, 'dp')
All inputs are finite; a program needn't handle non-finite values.
Results may differ from a plain program's by a relative error of at most 0.0057.
Values may be sent and summed in bfloat16 or wider, within the bound.
No kernel may reach another device: no remote copies, remote signals or barrier semaphores. Data moves between devices by JAX's collectives and lax.ppermute only.
A program may use at most 256 MiB of HBM per device.

v0:
```python
from functools import partial

import jax
import jax.numpy as jnp
import numpy as np
from jax import lax
from jax.sharding import PartitionSpec as P

PARTNERS = 6


gelu_tanh = partial(jax.nn.gelu, approximate=True)


def swapped(value, axis, apart):
    mask = 2**apart
    pairs = [(source, source ^ mask) for source in range(lax.axis_size(axis))]
    return lax.ppermute(value, axis, pairs)


def neighbours(blocks):
    per_device = blocks.shape[1]
    result = [blocks]
    for bit_pos in range(PARTNERS - 1):
        distance = 1 << bit_pos
        if distance < per_device:
            result.append(blocks[:, np.arange(per_device) ^ distance, :])
        else:
            level = (distance // per_device).bit_length() - 1
            result.append(swapped(blocks, "feat", level))
    return result


def mix_layer(parts, weight):
    total = jnp.einsum("tnb,nbc->tnc", parts[0], weight[:, 0], preferred_element_type=jnp.float32)
    for which in range(1, PARTNERS):
        total = total + jnp.einsum(
            "tnb,nbc->tnc", parts[which], weight[:, which], preferred_element_type=jnp.float32
        )
    return total


def back_sum(delta, weight):
    per_device = delta.shape[1]
    total = (
        jnp.einsum("tnc,nbc->tnb", delta, weight[:, 0], preferred_element_type=jnp.float32)
        .astype(jnp.bfloat16)
        .astype(jnp.float32)
    )
    for bit_pos in range(PARTNERS - 1):
        distance = 1 << bit_pos
        term = jnp.einsum(
            "tnc,nbc->tnb", delta, weight[:, bit_pos + 1], preferred_element_type=jnp.float32
        ).astype(jnp.bfloat16)
        if distance < per_device:
            arrived = term[:, np.arange(per_device) ^ distance, :]
        else:
            level = (distance // per_device).bit_length() - 1
            arrived = swapped(term, "feat", level)
        total = total + arrived.astype(jnp.float32)
    return total


def local(tokens, weight, cotangent):
    tok_rows = tokens.shape[0]
    per_device = weight.shape[0]
    block_width = weight.shape[2]
    inputs = tokens.reshape(tok_rows, per_device, block_width)
    parts = neighbours(inputs)
    z_value = mix_layer(parts, weight)
    output = gelu_tanh(z_value).astype(jnp.bfloat16)
    unused, pull_back = jax.vjp(gelu_tanh, z_value)
    delta = pull_back(cotangent.reshape(tok_rows, per_device, block_width).astype(jnp.float32))[
        0
    ].astype(jnp.bfloat16)
    local_all = jnp.stack(
        [
            jnp.einsum("tnb,tnc->nbc", parts[which], delta, preferred_element_type=jnp.float32)
            for which in range(PARTNERS)
        ],
        axis=1,
    )
    weight_grad = lax.psum_scatter(local_all, "dp", scatter_dimension=2, tiled=True)
    input_grad = back_sum(delta, weight).astype(jnp.bfloat16)
    return (
        output.reshape(tok_rows, per_device * block_width),
        input_grad.reshape(tok_rows, per_device * block_width),
        weight_grad,
    )


def solution(mesh):
    return jax.shard_map(
        local,
        mesh=mesh,
        in_specs=(P("dp", "feat"), P("feat", None, None, None), P("dp", "feat")),
        out_specs=(P("dp", "feat"), P("dp", "feat"), P("feat", None, "dp", None)),
        check_vma=False,
    )
```

profile of v0, /device:TPU:0, one launch (start us, length us, event | category | flops | bytes accessed | tf_op | source)
XLA Modules:
  0.0 630.3 jit_solution(17478268562484229325)
XLA Ops:
  7.2 0.0 reduce-scatter.2.cloned.1.call-start
  7.2 6.4 %copy.93 = bf16[512,4096]{0,1:T(8,128)(2,1)} copy(bf16[512,4096]{1,0:T(8,128)(2,1)} %param.15) | data formatting | bytes 8388608 | tf_op args[0]
  13.6 0.0 copy-start.11
  13.6 6.5 %copy.102 = bf16[512,8,512]{2,0,1:T(8,128)(2,1)} copy(bf16[512,8,512]{0,2,1:T(8,128)(2,1)} %bitcast.155) | data formatting | bytes 8388608 | tf_op jit(solution)/shard_map/reshape | solution.py:68
  20.1 3.0 collective-permute-start
  23.1 2.6 collective-permute-start.1
  25.7 0.0 copy-done.11
  25.7 0.0 copy-done.12
  25.7 5.0 gather_fusion.2
  30.7 0.0 copy-start.10
  30.7 5.0 gather_fusion.1
  35.7 0.0 copy-done.10
  35.7 0.0 copy-start.9
  35.7 5.0 gather_fusion
  40.7 0.0 copy-done.9
  40.7 7.1 %copy.105 = f32[512,4096]{0,1:T(8,128)} copy(bf16[512,4096]{1,0:T(8,128)(2,1)} %param.17) | data formatting | bytes 12582912 | tf_op jit(solution)/shard_map/convert_element_type | solution.py:73
  47.8 9.2 %fusion.31 = f32[8,512,512]{2,1,0:T(8,128)} fusion(bf16[512,8,512]{0,2,1:T(8,128)(2,1)} %bitcast.159, bf16[8,6,512,512]{3,2,1,0:T(8,128)(2,1)} %param.16), kind=kOutput, calls=%fused_computation.52 | convolution fusion | flops 2147483648 | bytes 16777216 | tf_op jit(solution)/shard_map/tnb,nbc->tnc/dot_general | solution.py:35
  57.0 0.0 copy-done.3
  57.0 7.9 %fusion.19 = f32[8,512,512]{1,2,0:T(8,128)} fusion(bf16[8,512,512]{1,2,0:T(8,128)(2,1)S(1)} %copy-done.3, bf16[8,6,512,512]{3,2,1,0:T(8,128)(2,1)} %param.16), kind=kOutput, calls=%fused_computation.40 | convolution fusion | flops 2147483648 | bytes 16777216 | tf_op jit(solution)/shard_map/tnb,nbc->tnc/dot_general | solution.py:37
  65.0 0.0 copy-done.5
  65.0 7.9 %fusion.23 = f32[8,512,512]{1,2,0:T(8,128)} fusion(bf16[8,512,512]{1,2,0:T(8,128)(2,1)S(1)} %copy-done.5, bf16[8,6,512,512]{3,2,1,0:T(8,128)(2,1)} %param.16), kind=kOutput, calls=%fused_computation.44 | convolution fusion | flops 2147483648 | bytes 16777216 | tf_op jit(solution)/shard_map/tnb,nbc->tnc/dot_general | solution.py:37
  72.9 0.0 copy-done.7
  72.9 7.8 %fusion.27 = f32[8,512,512]{1,2,0:T(8,128)} fusion(bf16[8,512,512]{1,2,0:T(8,128)(2,1)S(1)} %copy-done.7, bf16[8,6,512,512]{3,2,1,0:T(8,128)(2,1)} %param.16), kind=kOutput, calls=%fused_computation.48 | convolution fusion | flops 2147483648 | bytes 16777216 | tf_op jit(solution)/shard_map/tnb,nbc->tnc/dot_general | solution.py:37
  80.7 123.0 %collective-permute-done = bf16[512,8,512]{2,0,1:T(8,128)(2,1)} collective-permute-done((bf16[512,8,512]{2,0,1:T(8,128)(2,1)}, bf16[512,8,512]{2,0,1:T(8,128)(2,1)}, u32[]{:S(2)}, u32[]{:S(2)}) %collective-permute-start) | collective-permute-done | bytes 4194336 | tf_op jit(solution)/shard_map/ppermute | solution.py:18
  203.8 9.2 %fusion.15 = f32[8,512,512]{2,1,0:T(8,128)} fusion(bf16[512,8,512]{2,0,1:T(8,128)(2,1)} %collective-permute-done, bf16[8,6,512,512]{3,2,1,0:T(8,128)(2,1)} %param.16), kind=kOutput, calls=%fused_computation.36 | convolution fusion | flops 2147483648 | bytes 16777216 | tf_op jit(solution)/shard_map/tnb,nbc->tnc/dot_general | solution.py:37
  213.0 0.0 collective-permute-done.1
  213.0 24.3 %fusion.6 = (bf16[512,8,512]{0,2,1:T(8,128)(2,1)}, bf16[512,8,512]{0,2,1:T(8,128)(2,1)}) fusion(f32[512,8,512]{0,2,1:T(8,128)} %bitcast.161, bf16[512,8,512]{2,0,1:T(8,128)(2,1)} %collective-permute-done.1, bf16[8,6,512,512]{3,2,1,0:T(8,128)(2,1)} %param.16, f32[8,512,512]{2,1,0:T(8,128)} %fusion.15, f32[8,512,512]{1,2,0:T(8,128)} %fusion.19, ...), kind=kOutput, calls=%fused_computation.14 | convolution fusion | flops 2204106752 | bytes 67108864 | tf_op jit(solution)/shard_map/tnb,nbc->tnc/dot_general | solution.py:37
  237.3 0.0 copy-done
  237.3 0.0 copy-start.1
  237.3 0.0 copy-start.8
  237.3 7.9 %bitcast_dynamic-update-slice_fusion.2 = f32[8,6,512,512]{2,3,0,1:T(8,128)} fusion(bf16[512,8,512]{0,2,1:T(8,128)(2,1)} %get-tuple-element.12, bf16[512,8,512]{0,2,1:T(8,128)(2,1)S(1)} %bitcast.160), kind=kOutput, calls=%fused_computation.17 | convolution fusion | flops 2147483648 | bytes 16777216 | tf_op jit(solution)/shard_map/tnb,tnc->nbc/dot_general | solution.py:78
  245.3 0.0 copy-done.1
  245.3 0.0 copy-done.8
  245.3 5.6 bitcast_dynamic-update-slice_fusion.5
  250.9 0.0 copy-done.6
  250.9 5.7 bitcast_dynamic-update-slice_fusion.4
  256.6 0.0 copy-done.4
  256.6 5.6 bitcast_dynamic-update-slice_fusion.3
  262.2 7.8 %bitcast_dynamic-update-slice_fusion.1 = f32[8,6,512,512]{2,3,0,1:T(8,128)} fusion(f32[8,6,512,512]{2,3,0,1:T(8,128)} %bitcast_dynamic-update-slice_fusion.3, bf16[512,8,512]{0,2,1:T(8,128)(2,1)S(1)} %copy-done.1, bf16[512,8,512]{2,0,1:T(8,128)(2,1)} %collective-permute-done), kind=kOutput, calls=%fused_computation.16 | convolution fusion | flops 2147483648 | bytes 16777216 | tf_op jit(solution)/shard_map/tnb,tnc->nbc/dot_general | solution.py:78
  270.0 7.9 %bitcast_dynamic-update-slice_fusion = f32[8,6,512,512]{2,3,0,1:T(8,128)} fusion(f32[8,6,512,512]{2,3,0,1:T(8,128)} %bitcast_dynamic-update-slice_fusion.1, bf16[512,8,512]{0,2,1:T(8,128)(2,1)S(1)} %copy-done.1, bf16[512,8,512]{2,0,1:T(8,128)(2,1)} %collective-permute-done.1), kind=kOutput, calls=%fused_computation.15 | convolution fusion | flops 2147483648 | bytes 16777216 | tf_op jit(solution)/shard_map/tnb,tnc->nbc/dot_general | solution.py:78
  277.9 49.8 %copy.130 = f32[8,6,512,512]{3,0,1,2:T(8,128)} copy(f32[8,6,512,512]{2,3,0,1:T(8,128)} %bitcast_dynamic-update-slice_fusion) | data formatting | bytes 100663296 | tf_op jit(solution)/shard_map/stack | solution.py:76
  327.7 0.0 reduce-scatter.2.cloned.1.call-update
  327.7 0.0 copy-start.2
  327.8 8.1 %convert_bitcast_fusion.1 = bf16[512,8,512]{0,2,1:T(8,128)(2,1)} fusion(bf16[512,8,512]{0,2,1:T(8,128)(2,1)} %get-tuple-element.12, bf16[8,6,512,512]{3,2,1,0:T(8,128)(2,1)} %param.16), kind=kOutput, calls=%fused_computation.64 | convolution fusion | flops 2149580800 | bytes 12582912 | tf_op jit(solution)/shard_map/tnc,nbc->tnb/dot_general | solution.py:52
  335.9 0.0 copy-done.2
  335.9 8.2 %convert_bitcast_fusion = bf16[512,8,512]{0,2,1:T(8,128)(2,1)} fusion(bf16[512,8,512]{0,2,1:T(8,128)(2,1)S(1)} %copy-done.2, bf16[8,6,512,512]{3,2,1,0:T(8,128)(2,1)} %param.16), kind=kOutput, calls=%fused_computation.63 | convolution fusion | flops 2149580800 | bytes 12582912 | tf_op jit(solution)/shard_map/tnc,nbc->tnb/dot_general | solution.py:52
  344.1 0.0 collective-permute-start.2
  344.1 3.3 collective-permute-start.3
  347.3 8.2 %convert_bitcast_fusion.3 = bf16[512,8,512]{2,0,1:T(8,128)(2,1)} fusion(bf16[512,8,512]{0,2,1:T(8,128)(2,1)S(1)} %copy-done.2, bf16[8,6,512,512]{3,2,1,0:T(8,128)(2,1)} %param.16), kind=kOutput, calls=%fused_computation.66 | convolution fusion | flops 2149580800 | bytes 12582912 | tf_op jit(solution)/shard_map/tnc,nbc->tnb/dot_general | solution.py:52
  355.6 6.6 %gather_fusion.4 = bf16[8,512,512]{2,1,0:T(8,128)(2,1)} fusion(bf16[512,8,512]{2,0,1:T(8,128)(2,1)} %convert_bitcast_fusion.3, s32[1024]{0:T(1024)S(1)} %get-tuple-element.15), kind=kCustom, calls=%fused_computation.4 | custom fusion | bytes 8388640 | tf_op jit(solution)/shard_map/gather | solution.py:56
  362.2 6.9 %copy.113 = bf16[8,512,512]{1,2,0:T(8,128)(2,1)} copy(bf16[8,512,512]{2,1,0:T(8,128)(2,1)} %gather_fusion.4) | data formatting | bytes 8388608 | tf_op jit(solution)/shard_map/gather | solution.py:56
  369.1 10.5 %convert_bitcast_fusion.2 = bf16[512,8,512]{2,0,1:T(8,128)(2,1)} fusion(bf16[512,8,512]{0,2,1:T(8,128)(2,1)} %get-tuple-element.12, bf16[8,6,512,512]{3,2,1,0:T(8,128)(2,1)} %param.16), kind=kOutput, calls=%fused_computation.65 | convolution fusion | flops 2149580800 | bytes 12582912 | tf_op jit(solution)/shard_map/tnc,nbc->tnb/dot_general | solution.py:52
  379.5 6.6 %gather_fusion.5 = bf16[8,512,512]{2,1,0:T(8,128)(2,1)} fusion(bf16[512,8,512]{2,0,1:T(8,128)(2,1)} %convert_bitcast_fusion.2, s32[1024]{0:T(1024)S(1)} %get-tuple-element.14), kind=kCustom, calls=%fused_computation.5 | custom fusion | bytes 8388640 | tf_op jit(solution)/shard_map/gather | solution.py:56
  386.1 6.9 %copy.116 = bf16[8,512,512]{1,2,0:T(8,128)(2,1)} copy(bf16[8,512,512]{2,1,0:T(8,128)(2,1)} %gather_fusion.5) | data formatting | bytes 8388608 | tf_op jit(solution)/shard_map/gather | solution.py:56
  393.1 8.0 %convert_bitcast_fusion.4 = bf16[512,8,512]{2,0,1:T(8,128)(2,1)} fusion(bf16[512,8,512]{0,2,1:T(8,128)(2,1)} %get-tuple-element.12, bf16[8,6,512,512]{3,2,1,0:T(8,128)(2,1)} %param.16), kind=kOutput, calls=%fused_computation.67 | convolution fusion | flops 2149580800 | bytes 12582912 | tf_op jit(solution)/shard_map/tnc,nbc->tnb/dot_general | solution.py:52
  401.1 5.2 gather_fusion.3
  406.3 6.8 %copy.110 = bf16[8,512,512]{1,2,0:T(8,128)(2,1)} copy(bf16[8,512,512]{2,1,0:T(8,128)(2,1)} %gather_fusion.3) | data formatting | bytes 8388608 | tf_op jit(solution)/shard_map/gather | solution.py:56
  413.1 6.4 %copy.131 = bf16[512,4096]{1,0:T(8,128)(2,1)} copy(bf16[512,4096]{0,1:T(8,128)(2,1)} %bitcast.162) | data formatting | bytes 8388608
  419.5 105.5 %collective-permute-done.2 = bf16[512,8,512]{0,2,1:T(8,128)(2,1)} collective-permute-done((bf16[512,8,512]{0,2,1:T(8,128)(2,1)}, bf16[512,8,512]{0,2,1:T(8,128)(2,1)}, u32[]{:S(2)}, u32[]{:S(2)}) %collective-permute-start.2) | collective-permute-done | bytes 4194336 | tf_op jit(solution)/shard_map/ppermute | solution.py:18
  525.0 2.0 collective-permute-done.3
  527.0 15.5 %fusion.8 = bf16[512,8,512]{0,2,1:T(8,128)(2,1)} fusion(bf16[8,512,512]{1,2,0:T(8,128)(2,1)} %copy.116, bf16[8,512,512]{1,2,0:T(8,128)(2,1)} %copy.113, bf16[8,512,512]{1,2,0:T(8,128)(2,1)} %copy.110, bf16[512,8,512]{0,2,1:T(8,128)(2,1)} %collective-permute-done.3, bf16[512,8,512]{0,2,1:T(8,128)(2,1)} %collective-permute-done.2, ...), kind=kOutput, calls=%fused_computation.23 | convolution fusion | flops 2174746624 | bytes 33554432 | tf_op jit(solution)/shard_map/tnc,nbc->tnb/dot_general | solution.py:46
  542.5 6.4 %copy.132 = bf16[512,4096]{1,0:T(8,128)(2,1)} copy(bf16[512,4096]{0,1:T(8,128)(2,1)} %bitcast.163) | data formatting | bytes 8388608
  548.9 65.2 %reduce-scatter.2.cloned.1.call-done = f32[8,6,64,512]{3,0,1,2:T(8,128)} async-done(((f32[8,6,512,512]{3,0,1,2:T(8,128)}), f32[8,6,64,512]{3,0,1,2:T(8,128)}) %reduce-scatter.2.cloned.1.call-update) | async-done | bytes 6291472 | tf_op jit(solution)/shard_map/reduce_scatter | solution.py:83
  614.1 9.1 %copy.133 = f32[8,6,64,512]{3,2,1,0:T(8,128)} copy(f32[8,6,64,512]{3,0,1,2:T(8,128)} %reduce-scatter.2.cloned.1.call-done) | data formatting | bytes 12582912
  (9 shorter events, 0.0 us)
Async XLA Ops:
  7.2 607.0 %reduce-scatter.2.cloned.1.call-start = ((), (), s32[]{:S(2)}) async-start(), calls=%async_computation.1 | async-start | bytes 56623104 | tf_op jit(solution)/shard_map/reduce_scatter | solution.py:83
  13.6 12.1 %copy-start.11 = (s32[8]{0:T(128)S(1)}, s32[8]{0:T(128)}, u32[]{:S(2)}) copy-start(s32[8]{0:T(128)} %constant.30) | copy-start | bytes 100
  13.6 12.1 %copy-start.12 = (s32[8]{0:T(128)S(1)}, s32[8]{0:T(128)}, u32[]{:S(2)}) copy-start(s32[8]{0:T(128)} %constant.31) | copy-start | bytes 100
  20.1 183.7 %collective-permute-start = (bf16[512,8,512]{2,0,1:T(8,128)(2,1)}, bf16[512,8,512]{2,0,1:T(8,128)(2,1)}, u32[]{:S(2)}, u32[]{:S(2)}) collective-permute-start(bf16[512,8,512]{2,0,1:T(8,128)(2,1)} %copy.102), channel_id=1, source_target_pairs={{0,1},{1,0},{2,3},{3,2},{4,5},{5,4},{6,7},{7,6},{8,9},{9,8},{10,11... | collective-permute-start | bytes 12582920 | tf_op jit(solution)/shard_map/ppermute | solution.py:18
  23.1 189.9 %collective-permute-start.1 = (bf16[512,8,512]{2,0,1:T(8,128)(2,1)}, bf16[512,8,512]{2,0,1:T(8,128)(2,1)}, u32[]{:S(2)}, u32[]{:S(2)}) collective-permute-start(bf16[512,8,512]{2,0,1:T(8,128)(2,1)} %copy.102), channel_id=1, source_target_pairs={{0,2},{1,3},{2,0},{3,1},{4,6},{5,7},{6,4},{7,5},{8,10},{9,11},{10,... | collective-permute-start | bytes 12582920 | tf_op jit(solution)/shard_map/ppermute | solution.py:18
  30.7 5.0 copy-start.10
  35.7 5.0 copy-start.9
  47.8 9.2 %copy-start.3 = (bf16[8,512,512]{1,2,0:T(8,128)(2,1)S(1)}, bf16[8,512,512]{1,2,0:T(8,128)(2,1)}, u32[]{:S(2)}) copy-start(bf16[8,512,512]{1,2,0:T(8,128)(2,1)} %gather_fusion.2) | copy-start | bytes 12582916
  57.0 7.9 %copy-start.5 = (bf16[8,512,512]{1,2,0:T(8,128)(2,1)S(1)}, bf16[8,512,512]{1,2,0:T(8,128)(2,1)}, u32[]{:S(2)}) copy-start(bf16[8,512,512]{1,2,0:T(8,128)(2,1)} %gather_fusion.1) | copy-start | bytes 12582916
  65.0 8.0 %copy-start.7 = (bf16[8,512,512]{1,2,0:T(8,128)(2,1)S(1)}, bf16[8,512,512]{1,2,0:T(8,128)(2,1)}, u32[]{:S(2)}) copy-start(bf16[8,512,512]{1,2,0:T(8,128)(2,1)} %gather_fusion) | copy-start | bytes 12582916
  213.0 24.3 %copy-start = (bf16[512,4096]{0,1:T(8,128)(2,1)S(1)}, bf16[512,4096]{0,1:T(8,128)(2,1)}, u32[]{:S(2)}) copy-start(bf16[512,4096]{0,1:T(8,128)(2,1)} %copy.93) | copy-start | bytes 12582916
  237.3 8.0 %copy-start.1 = (bf16[512,8,512]{0,2,1:T(8,128)(2,1)S(1)}, bf16[512,8,512]{0,2,1:T(8,128)(2,1)}, u32[]{:S(2)}) copy-start(bf16[512,8,512]{0,2,1:T(8,128)(2,1)} %get-tuple-element.12) | copy-start | bytes 12582916
  237.3 8.0 %copy-start.8 = (bf16[8,512,512]{1,2,0:T(8,128)(2,1)S(1)}, bf16[8,512,512]{1,2,0:T(8,128)(2,1)}, u32[]{:S(2)}) copy-start(bf16[8,512,512]{1,2,0:T(8,128)(2,1)} %gather_fusion) | copy-start | bytes 12582916
  245.3 5.6 copy-start.6
  250.9 5.7 copy-start.4
  327.7 8.1 %copy-start.2 = (bf16[512,8,512]{0,2,1:T(8,128)(2,1)S(1)}, bf16[512,8,512]{0,2,1:T(8,128)(2,1)}, u32[]{:S(2)}) copy-start(bf16[512,8,512]{0,2,1:T(8,128)(2,1)} %get-tuple-element.12) | copy-start | bytes 12582916
  344.1 180.9 %collective-permute-start.2 = (bf16[512,8,512]{0,2,1:T(8,128)(2,1)}, bf16[512,8,512]{0,2,1:T(8,128)(2,1)}, u32[]{:S(2)}, u32[]{:S(2)}) collective-permute-start(bf16[512,8,512]{0,2,1:T(8,128)(2,1)} %convert_bitcast_fusion.1), channel_id=1, source_target_pairs={{0,1},{1,0},{2,3},{3,2},{4,5},{5,4},{6,7},{7,6},{8,9},{9,8},{10,11... | collective-permute-start | bytes 12582920 | tf_op jit(solution)/shard_map/ppermute | solution.py:18
  344.1 183.0 %collective-permute-start.3 = (bf16[512,8,512]{0,2,1:T(8,128)(2,1)}, bf16[512,8,512]{0,2,1:T(8,128)(2,1)}, u32[]{:S(2)}, u32[]{:S(2)}) collective-permute-start(bf16[512,8,512]{0,2,1:T(8,128)(2,1)} %convert_bitcast_fusion), channel_id=1, source_target_pairs={{0,2},{1,3},{2,0},{3,1},{4,6},{5,7},{6,4},{7,5},{8,10},{9,11},{10,... | collective-permute-start | bytes 12582920 | tf_op jit(solution)/shard_map/ppermute | solution.py:18
Sparse Core Ops, SparseCore 0:
  327.9 286.2 reduce-scatter.1
where the time goes:
time: 642 us; the launch traced here: 630 us
  waiting for transfers between devices  296 us (46%)
  matrix products  165 us (26%)
  local copies, waits for them, and re-layouts  146 us (23%)
  between operations  14.3 us (2%)
  starting transfers between devices  8.94 us (1%)
    ppermute x4, waiting for transfers between devices, swapped(): return lax.ppermute(value, axis, pairs)  231 us
    reduce_scatter x1, waiting for transfers between devices, local(): lax.psum_scatter(local_all, 'dp', scatter_dimension=2, tiled=True)  65.2 us
    dot_general x5, matrix products, mix_layer(): jnp.einsum('tnb,nbc->tnc', parts[which], weight[:, which], preferred_elem...  57.2 us
    another operation x1, local copies, waits for them, and re-layouts, local(): jnp.stack([jnp.einsum('tnb,tnc->nbc', parts[which], delta, preferred_elem...  49.8 us
    dot_general x5, matrix products, back_sum(): jnp.einsum('tnc,nbc->tnb', delta, weight[:, bit_pos + 1], preferred_eleme...  43 us
    dot_general x6, matrix products, local(): jnp.einsum('tnb,tnc->nbc', parts[which], delta, preferred_element_type=jn...  40.5 us
    gather x6, local copies, waits for them, and re-layouts, back_sum(): arrived = term[:, np.arange(per_device) ^ distance, :]  39 us
    unnamed x30, local copies, waits for them, and re-layouts  28.4 us
  transfers between devices with their start and end apart: 5, of which 4 were waited for; matrix products, arithmetic and copies ran while one was open for 28% of the time, Pallas kernels for 0%

commit v1 on v0

v1 whole, which is shorter than its diff:
```python
from functools import partial

import jax
import jax.numpy as jnp
from jax import lax
from jax.experimental import pallas as pl
from jax.experimental.pallas import tpu as pltpu
from jax.sharding import PartitionSpec as P

VMEM_BYTES = 48 * 2**20
GELU_SCALE = 0.7978845608028654
GELU_CUBIC = 0.044715

any_spec = pl.BlockSpec(memory_space=pl.ANY)


def dot(left, right, contract):
    return lax.dot_general(left, right, (contract, ((), ())), preferred_element_type=jnp.float32)


def gelu_and_slope(value):
    square = value * value
    tanh = jnp.tanh(GELU_SCALE * (value + GELU_CUBIC * (square * value)))
    half = 0.5 * (1.0 + tanh)
    inner = GELU_SCALE * (1.0 + (3.0 * GELU_CUBIC) * square)
    return value * half, half + 0.5 * value * (1.0 - tanh * tanh) * inner


def swapped(value, level):
    mask = 1 << level
    pairs = [(source, source ^ mask) for source in range(lax.axis_size("feat"))]
    return lax.ppermute(value, "feat", pairs)


def block_step(partners, near, split, *refs):
    far = partners - near
    parts = refs[:partners]
    weight, cotangent = refs[partners : partners + 2]
    output, delta_out, grads = refs[-3 - far : -far] if far else refs[-3:]
    terms = refs[-far:] if far else ()
    total = dot(parts[0][...], weight[0, 0], ((1,), (0,)))
    for which in range(1, partners):
        total = total + dot(parts[which][...], weight[0, which], ((1,), (0,)))
    value, slope = gelu_and_slope(total)
    output[...] = value.astype(output.dtype)
    delta = (cotangent[...].astype(jnp.float32) * slope).astype(delta_out.dtype)
    delta_out[...] = delta
    for index in range(far):
        terms[index][...] = dot(delta, weight[0, near + index], ((1,), (1,))).astype(delta.dtype)
    for which in range(partners):
        grad = dot(parts[which][...], delta, ((0,), (0,))).astype(grads.dtype)
        grads[:, 0, which] = grad.reshape(split, grad.shape[0] // split, grad.shape[1])


def near_step(near, *refs):
    deltas, weights, total = refs[:near], refs[near : 2 * near], refs[-1]
    value = dot(deltas[0][...], weights[0][0, 0], ((1,), (1,)))
    for which in range(1, near):
        value = value + dot(deltas[which][...], weights[which][0, 0], ((1,), (1,)))
    total[...] = value


def last_step(far, *refs):
    value = refs[0][...]
    for index in range(far):
        value = value + refs[1 + index][...].astype(jnp.float32)
    refs[-1][...] = value.astype(refs[-1].dtype)


def local(tokens, weight, cotangent):
    rows = tokens.shape[0]
    blocks, partners, width = weight.shape[:3]
    near = blocks.bit_length()
    far = partners - near
    split = lax.axis_size("dp")
    shard = width // split
    sixteen = tokens.dtype
    params = pltpu.CompilerParams(vmem_limit_bytes=VMEM_BYTES)

    def column(index):
        return pl.BlockSpec((rows, width), lambda *_: (0, index))

    groups, first = [], 0
    while first < blocks:
        size = max(first, 1)
        groups.append((first, size))
        first += size

    arrived = []
    for index, (first, size) in enumerate(groups):
        piece = tokens[:, first * width : (first + size) * width]
        if index >= 3:
            piece, arrived[index - 3] = lax.optimization_barrier((piece, arrived[index - 3]))
        arrived.append([swapped(piece, level) for level in reversed(range(far))][::-1])

    halves = 2 if blocks > 1 else 1
    per_half = blocks // halves
    output = delta = None
    received, scattered = [], []
    for (first, size), pieces in zip(groups, arrived):
        for block in range(first, first + size):
            if block % per_half == 0:
                grads = None
            at = block % per_half
            parts = [tokens] + [tokens] * (near - 1) + list(pieces)
            specs = [column(block)] + [column(block ^ (1 << bit)) for bit in range(near - 1)]
            specs += [column(block - first)] * far
            operands = parts + [weight, cotangent]
            specs += [
                pl.BlockSpec((1, partners, width, width), lambda *_, block=block: (block, 0, 0, 0)),
                column(block),
            ]
            aliases = {}
            for where, chained in enumerate((output, delta, grads)):
                if chained is not None:
                    aliases[len(operands)] = where
                    operands.append(chained)
                    specs.append(any_spec)
            moved = 2 * (3 * partners * width * width + rows * width * (partners + far + 3))
            output, delta, grads, *terms = pl.pallas_call(
                partial(block_step, partners, near, split),
                grid=(1,),
                in_specs=specs,
                out_specs=[
                    column(block),
                    column(block),
                    pl.BlockSpec((split, 1, partners, shard, width), lambda *_, at=at: (0, at, 0, 0, 0)),
                ]
                + [column(0)] * far,
                out_shape=[
                    jax.ShapeDtypeStruct(tokens.shape, sixteen),
                    jax.ShapeDtypeStruct(tokens.shape, sixteen),
                    jax.ShapeDtypeStruct((split, per_half, partners, shard, width), sixteen),
                ]
                + [jax.ShapeDtypeStruct((rows, width), sixteen)] * far,
                input_output_aliases=aliases,
                compiler_params=params,
                cost_estimate=pl.CostEstimate(
                    flops=2 * rows * width * width * (2 * partners + far),
                    bytes_accessed=moved,
                    transcendentals=rows * width,
                ),
                name="block_step",
            )(*operands)
            received.append([swapped(terms[level], level) for level in reversed(range(far))][::-1])
            if at == per_half - 1:
                scattered.append(lax.psum_scatter(grads, "dp", scatter_dimension=0, tiled=False))

    near_total = pl.pallas_call(
        partial(near_step, near),
        grid=(blocks,),
        in_specs=[
            pl.BlockSpec((rows, width), lambda m, mask=mask: (0, m ^ mask))
            for mask in [0] + [1 << bit for bit in range(near - 1)]
        ]
        + [
            pl.BlockSpec((1, 1, width, width), lambda m, mask=mask, which=which: (m ^ mask, which, 0, 0))
            for which, mask in enumerate([0] + [1 << bit for bit in range(near - 1)])
        ],
        out_specs=pl.BlockSpec((rows, width), lambda m: (0, m)),
        out_shape=jax.ShapeDtypeStruct(tokens.shape, jnp.float32),
        compiler_params=params,
        cost_estimate=pl.CostEstimate(
            flops=2 * rows * width * width * near * blocks,
            bytes_accessed=blocks * near * 2 * width * (rows + width) + 4 * rows * width * blocks,
            transcendentals=0,
        ),
        name="near_step",
    )(*[delta] * near, *[weight] * near)

    input_grad = None
    for block in range(blocks):
        operands = [near_total] + received[block]
        specs = [column(block)] + [column(0)] * far
        aliases = {}
        if input_grad is not None:
            aliases[len(operands)] = 0
            operands.append(input_grad)
            specs.append(any_spec)
        input_grad = pl.pallas_call(
            partial(last_step, far),
            grid=(1,),
            in_specs=specs,
            out_specs=column(block),
            out_shape=jax.ShapeDtypeStruct(tokens.shape, sixteen),
            input_output_aliases=aliases,
            compiler_params=params,
            cost_estimate=pl.CostEstimate(
                flops=rows * width * far, bytes_accessed=rows * width * (6 + 2 * far), transcendentals=0
            ),
            name="last_step",
        )(*operands)

    weight_grad = jnp.concatenate(scattered, axis=0).astype(jnp.float32)
    return output, input_grad, weight_grad


def solution(mesh):
    return jax.shard_map(
        local,
        mesh=mesh,
        in_specs=(P("dp", "feat"), P("feat", None, None, None), P("dp", "feat")),
        out_specs=(P("dp", "feat"), P("dp", "feat"), P("feat", None, "dp", None)),
        check_vma=False,
    )
```

time: 642 us -> 466 us (0.73); the launches traced: 630 us -> 465 us
  matrix products: 165 us -> 0 us
  local copies, waits for them, and re-layouts: 146 us -> 12.1 us
  Pallas kernels: 0 us -> 104 us
  starting transfers between devices: 8.94 us -> 24.2 us
  waiting for transfers between devices: 296 us -> 306 us
    dot_general x18 -> x0, matrix products: 165 us -> none  [the longest x5 57.2 us: mix_layer(): jnp.einsum('tnb,nbc->tnc', parts[which], weight[:, which], preferred_elem...]
    pallas_call x0 -> x17, Pallas kernels: none -> 104 us  [the longest x8 71.8 us: local(): pl.pallas_call(partial(block_step, partners, near, split), grid=(1,), in_...]
    ppermute x4 -> x24, waiting for transfers between devices: 231 us -> 306 us  [swapped(): return lax.ppermute(value, 'feat', pairs)]
    reduce_scatter x1 -> x2, waiting for transfers between devices: 65.2 us -> 0.01 us  [local(): lax.psum_scatter(grads, 'dp', scatter_dimension=0, tiled=False)]
    gather x9 -> x0, local copies, waits for them, and re-layouts: 54 us -> none  [the longest x6 39 us: back_sum(): arrived = term[:, np.arange(per_device) ^ distance, :]]
    another operation x1 -> x0, local copies, waits for them, and re-layouts: 49.8 us -> none  [local(): jnp.stack([jnp.einsum('tnb,tnc->nbc', parts[which], delta, preferred_elem...]
    unnamed x30 -> x24, local copies, waits for them, and re-layouts: 28.4 us -> 7.85 us
    ppermute x4 -> x24, starting transfers between devices: 8.9 us -> 24.1 us  [swapped(): return lax.ppermute(value, 'feat', pairs)]
  transfers between devices with their start and end apart: 5 -> 26, of which waited for: 4 -> 17; matrix products, arithmetic and copies ran while one was open for 28% -> 1% of each run, Pallas kernels for 0% -> 18%
where the time goes in v1:
time: 466 us; the launch traced here: 465 us
  waiting for transfers between devices  306 us (66%)
  Pallas kernels  104 us (22%)
  starting transfers between devices  24.2 us (5%)
  between operations  14.1 us (3%)
  local copies, waits for them, and re-layouts  12.1 us (3%)
  other arithmetic  4.99 us (1%)
    ppermute x24, waiting for transfers between devices, swapped(): return lax.ppermute(value, 'feat', pairs)  306 us
    pallas_call x8, Pallas kernels, local(): pl.pallas_call(partial(block_step, partners, near, split), grid=(1,), in_...  71.8 us
    ppermute x24, starting transfers between devices, swapped(): return lax.ppermute(value, 'feat', pairs)  24.1 us
    pallas_call x8, Pallas kernels, local(): pl.pallas_call(partial(last_step, far), grid=(1,), in_specs=specs, out_sp...  17.4 us
    pallas_call x1, Pallas kernels, local(): pl.pallas_call(partial(near_step, near), grid=(blocks,), in_specs=[pl.Blo...  15.1 us
  transfers between devices with their start and end apart: 26, of which 17 were waited for; matrix products, arithmetic and copies ran while one was open for 1% of the time, Pallas kernels for 18%

profile of v1, /device:TPU:0, one launch (start us, length us, event | category | flops | bytes accessed | tf_op | source)
XLA Modules:
  0.0 465.3 jit_solution(3530791731185349805)
XLA Ops:
  7.2 1.4 fusion
  8.7 4.1 collective-permute-start.1
  12.8 1.6 collective-permute-start
  14.3 1.3 slice.14
  15.6 0.4 collective-permute-start.5
  16.0 0.2 collective-permute-start.4
  16.2 2.8 collective-permute-start.7
  19.1 18.6 %collective-permute-done.1.refs_5_ = bf16[512,512]{1,0:T(8,128)(2,1)S(1)} collective-permute-done((bf16[512,512]{1,0:T(8,128)(2,1)S(1)}, bf16[512,512]{1,0:T(8,128)(2,1)S(1)}, u32[]{:S(2)}, u32[]{:S(2)}) %collective-permute-start.1) | collective-permute-done | bytes 524320 | tf_op jit(solution)/shard_map/ppermute | solution.py:32
  37.7 1.6 slice.12
  39.3 8.8 %block_step.8 = (bf16[512,4096]{1,0:T(8,128)(2,1)}, bf16[512,4096]{1,0:T(8,128)(2,1)}, bf16[8,4,6,64,512]{4,3,2,1,0:T(8,128)(2,1)}, bf16[512,512]{1,0:T(8,128)(2,1)S(1)}, bf16[512,512]{1,0:T(8,128)(2,1)S(1)}) custom-call(bf16[512,4096]{1,0:T(8,128)(2,1)} %refs_3_.15, bf16[512,4096]{1,0:T(8,128)(2,1)} %refs_3_.15, bf16[512,4096]{1,0:T(8,128)(2,1)} %refs_3_.15, ...), custom_call_target="tpu_custom_call" | custom-call | flops 3758096384 | bytes 15204352 | tf_op jit(solution)/shard_map/block_step/pallas_call | solution.py:120
  48.1 55.5 %collective-permute-done.7.refs_5_ = bf16[512,512]{1,0:T(8,128)(2,1)S(1)} collective-permute-done((bf16[512,512]{1,0:T(8,128)(2,1)S(1)}, bf16[512,512]{1,0:T(8,128)(2,1)S(1)}, u32[]{:S(2)}, u32[]{:S(2)}) %collective-permute-start.7) | collective-permute-done | bytes 524320 | tf_op jit(solution)/shard_map/ppermute | solution.py:32
  103.5 0.1 collective-permute-done.6.refs_4_
  103.6 9.0 %block_step.9 = (bf16[512,4096]{1,0:T(8,128)(2,1)}, bf16[512,4096]{1,0:T(8,128)(2,1)}, bf16[8,4,6,64,512]{4,3,2,1,0:T(8,128)(2,1)}, bf16[512,512]{1,0:T(8,128)(2,1)S(1)}, bf16[512,512]{1,0:T(8,128)(2,1)S(1)}) custom-call(bf16[512,4096]{1,0:T(8,128)(2,1)} %refs_3_.15, ...), custom_call_target="tpu_custom_call", output_to_operand_aliasing={{0}: (8, {}), {1}: (9, {}), {2}: (10, {})} | custom-call | flops 3758096384 | bytes 15204352 | tf_op jit(solution)/shard_map/block_step/pallas_call | solution.py:120
  112.6 0.8 copy-done.10
  113.4 9.1 %block_step.10 = (bf16[512,4096]{1,0:T(8,128)(2,1)}, bf16[512,4096]{1,0:T(8,128)(2,1)}, bf16[8,4,6,64,512]{4,3,2,1,0:T(8,128)(2,1)}, bf16[512,512]{1,0:T(8,128)(2,1)S(1)}, bf16[512,512]{1,0:T(8,128)(2,1)S(1)}) custom-call(bf16[512,4096]{1,0:T(8,128)(2,1)} %refs_3_.15, ...), custom_call_target="tpu_custom_call", output_to_operand_aliasing={{0}: (8, {}), {1}: (9, {}), {2}: (10, {})} | custom-call | flops 3758096384 | bytes 15204352 | tf_op jit(solution)/shard_map/block_step/pallas_call | solution.py:120
  122.6 0.8 copy-done.2
  123.4 9.1 %block_step.11 = (bf16[512,4096]{1,0:T(8,128)(2,1)}, bf16[512,4096]{1,0:T(8,128)(2,1)}, bf16[8,4,6,64,512]{4,3,2,1,0:T(8,128)(2,1)}, bf16[512,512]{1,0:T(8,128)(2,1)S(1)}, bf16[512,512]{1,0:T(8,128)(2,1)S(1)}) custom-call(bf16[512,4096]{1,0:T(8,128)(2,1)} %refs_3_.15, ...), custom_call_target="tpu_custom_call", output_to_operand_aliasing={{0}: (8, {}), {1}: (9, {}), {2}: (10, {})} | custom-call | flops 3758096384 | bytes 15204352 | tf_op jit(solution)/shard_map/block_step/pallas_call | solution.py:120
  132.4 0.8 copy-done.4
  133.2 0.8 copy-done.8
  134.1 0.0 reduce-scatter.5.cloned.1.call-start
  134.1 1.5 collective-permute-start.3
  135.7 2.4 collective-permute-start.2
  138.1 88.9 %collective-permute-done.3.refs_5_ = bf16[512,2048]{1,0:T(8,128)(2,1)S(1)} collective-permute-done((bf16[512,2048]{1,0:T(8,128)(2,1)}, bf16[512,2048]{1,0:T(8,128)(2,1)S(1)}, u32[]{:S(2)}, u32[]{:S(2)}) %collective-permute-start.3) | collective-permute-done | bytes 2097184 | tf_op jit(solution)/shard_map/ppermute | solution.py:32
  227.0 0.1 collective-permute-done.2.refs_4_
  227.1 9.0 %block_step.12 = (bf16[512,4096]{1,0:T(8,128)(2,1)}, bf16[512,4096]{1,0:T(8,128)(2,1)}, bf16[8,4,6,64,512]{4,3,2,1,0:T(8,128)(2,1)}, bf16[512,512]{1,0:T(8,128)(2,1)S(1)}, bf16[512,512]{1,0:T(8,128)(2,1)S(1)}) custom-call(bf16[512,4096]{1,0:T(8,128)(2,1)} %refs_3_.15, bf16[512,4096]{1,0:T(8,128)(2,1)} %refs_3_.15, ...), custom_call_target="tpu_custom_call", output_to_operand_aliasing={{0}: (8, {}), {1}: (9, {})} | custom-call | flops 3758096384 | bytes 15204352 | tf_op jit(solution)/shard_map/block_step/pallas_call | solution.py:120
  236.1 0.8 copy-done.6
  236.9 0.8 copy-done.9
  237.7 8.9 %block_step.13 = (bf16[512,4096]{1,0:T(8,128)(2,1)}, bf16[512,4096]{1,0:T(8,128)(2,1)}, bf16[8,4,6,64,512]{4,3,2,1,0:T(8,128)(2,1)}, bf16[512,512]{1,0:T(8,128)(2,1)S(1)}, bf16[512,512]{1,0:T(8,128)(2,1)S(1)}) custom-call(bf16[512,4096]{1,0:T(8,128)(2,1)} %refs_3_.15, ...), custom_call_target="tpu_custom_call", output_to_operand_aliasing={{0}: (8, {}), {1}: (9, {}), {2}: (10, {})} | custom-call | flops 3758096384 | bytes 15204352 | tf_op jit(solution)/shard_map/block_step/pallas_call | solution.py:120
  246.6 0.8 copy-done.5
  247.4 8.9 %block_step.14 = (bf16[512,4096]{1,0:T(8,128)(2,1)}, bf16[512,4096]{1,0:T(8,128)(2,1)}, bf16[8,4,6,64,512]{4,3,2,1,0:T(8,128)(2,1)}, bf16[512,512]{1,0:T(8,128)(2,1)S(1)}, bf16[512,512]{1,0:T(8,128)(2,1)S(1)}) custom-call(bf16[512,4096]{1,0:T(8,128)(2,1)} %refs_3_.15, ...), custom_call_target="tpu_custom_call", output_to_operand_aliasing={{0}: (8, {}), {1}: (9, {}), {2}: (10, {})} | custom-call | flops 3758096384 | bytes 15204352 | tf_op jit(solution)/shard_map/block_step/pallas_call | solution.py:120
  256.2 9.1 %block_step.15 = (bf16[512,4096]{1,0:T(8,128)(2,1)}, bf16[512,4096]{1,0:T(8,128)(2,1)}, bf16[8,4,6,64,512]{4,3,2,1,0:T(8,128)(2,1)}, bf16[512,512]{1,0:T(8,128)(2,1)S(1)}, bf16[512,512]{1,0:T(8,128)(2,1)S(1)}) custom-call(bf16[512,4096]{1,0:T(8,128)(2,1)} %refs_3_.15, ...), custom_call_target="tpu_custom_call", output_to_operand_aliasing={{0}: (8, {}), {1}: (9, {}), {2}: (10, {})} | custom-call | flops 3758096384 | bytes 15204352 | tf_op jit(solution)/shard_map/block_step/pallas_call | solution.py:120
  265.4 0.4 collective-permute-start.20
  265.8 3.4 collective-permute-start.21
  269.2 0.3 collective-permute-start.22
  269.5 0.9 collective-permute-start.23
  270.4 0.9 collective-permute-start.16
  271.3 29.3 %collective-permute-done.20.refs_1_ = bf16[512,512]{1,0:T(8,128)(2,1)S(1)} collective-permute-done((bf16[512,512]{1,0:T(8,128)(2,1)}, bf16[512,512]{1,0:T(8,128)(2,1)S(1)}, u32[]{:S(2)}, u32[]{:S(2)}) %collective-permute-start.20) | collective-permute-done | bytes 524320 | tf_op jit(solution)/shard_map/ppermute | solution.py:32
  300.6 1.4 collective-permute-start.18
  302.0 13.9 %collective-permute-done.22.refs_1_ = bf16[512,512]{1,0:T(8,128)(2,1)S(1)} collective-permute-done((bf16[512,512]{1,0:T(8,128)(2,1)}, bf16[512,512]{1,0:T(8,128)(2,1)S(1)}, u32[]{:S(2)}, u32[]{:S(2)}) %collective-permute-start.22) | collective-permute-done | bytes 524320 | tf_op jit(solution)/shard_map/ppermute | solution.py:32
  315.9 0.2 collective-permute-done.23.refs_2_
  316.1 1.0 collective-permute-start.14
  317.1 21.2 %collective-permute-done.16.refs_1_ = bf16[512,512]{1,0:T(8,128)(2,1)S(1)} collective-permute-done((bf16[512,512]{1,0:T(8,128)(2,1)}, bf16[512,512]{1,0:T(8,128)(2,1)S(1)}, u32[]{:S(2)}, u32[]{:S(2)}) %collective-permute-start.16) | collective-permute-done | bytes 524320 | tf_op jit(solution)/shard_map/ppermute | solution.py:32
  338.4 0.3 collective-permute-done.17.refs_2_
  338.6 1.0 collective-permute-start.12
  339.6 21.2 %collective-permute-done.18.refs_1_ = bf16[512,512]{1,0:T(8,128)(2,1)S(1)} collective-permute-done((bf16[512,512]{1,0:T(8,128)(2,1)}, bf16[512,512]{1,0:T(8,128)(2,1)S(1)}, u32[]{:S(2)}, u32[]{:S(2)}) %collective-permute-start.18) | collective-permute-done | bytes 524320 | tf_op jit(solution)/shard_map/ppermute | solution.py:32
  360.8 0.4 collective-permute-done.19.refs_2_
  361.2 0.9 collective-permute-start.8
  362.1 21.2 %collective-permute-done.14.refs_1_ = bf16[512,512]{1,0:T(8,128)(2,1)S(1)} collective-permute-done((bf16[512,512]{1,0:T(8,128)(2,1)}, bf16[512,512]{1,0:T(8,128)(2,1)S(1)}, u32[]{:S(2)}, u32[]{:S(2)}) %collective-permute-start.14) | collective-permute-done | bytes 524320 | tf_op jit(solution)/shard_map/ppermute | solution.py:32
  383.2 0.4 collective-permute-done.15.refs_2_
  383.7 0.8 collective-permute-start.10
  384.5 21.2 %collective-permute-done.12.refs_1_ = bf16[512,512]{1,0:T(8,128)(2,1)S(1)} collective-permute-done((bf16[512,512]{1,0:T(8,128)(2,1)}, bf16[512,512]{1,0:T(8,128)(2,1)S(1)}, u32[]{:S(2)}, u32[]{:S(2)}) %collective-permute-start.12) | collective-permute-done | bytes 524320 | tf_op jit(solution)/shard_map/ppermute | solution.py:32
  405.7 2.2 copy-done
  407.8 15.1 %near_step.1.refs_0_ = f32[512,4096]{1,0:T(8,128)} custom-call(bf16[512,4096]{1,0:T(8,128)(2,1)S(1)} %copy-done, bf16[512,4096]{1,0:T(8,128)(2,1)S(1)} %copy-done, bf16[512,4096]{1,0:T(8,128)(2,1)S(1)} %copy-done, bf16[512,4096]{1,0:T(8,128)(2,1)S(1)} %copy-done, bf16[8,6,512,512]{3,2,1,0:T(8,128)(2,1)} %refs_7_.17, bf16[8,6,512,512]{3,2,1,0:T(8,128)(2,1)} %refs_7_.17, ...), custom_call_target="tpu_custom_call" | custom-call | flops 8589934592 | bytes 41943040 | tf_op jit(solution)/shard_map/near_step/pallas_call | solution.py:149
  422.9 2.2 last_step.8.refs_3_
  425.1 2.2 last_step.9.refs_3_
  427.3 2.2 last_step.10.refs_3_
  429.4 2.2 last_step.11.refs_3_
  431.6 2.2 last_step.12.refs_3_
  433.8 2.2 last_step.13.refs_3_
  436.0 10.1 %collective-permute-done.10.refs_1_ = bf16[512,512]{1,0:T(8,128)(2,1)S(1)} collective-permute-done((bf16[512,512]{1,0:T(8,128)(2,1)S(1)}, bf16[512,512]{1,0:T(8,128)(2,1)S(1)}, u32[]{:S(2)}, u32[]{:S(2)}) %collective-permute-start.10) | collective-permute-done | bytes 524320 | tf_op jit(solution)/shard_map/ppermute | solution.py:32
  446.1 3.0 collective-permute-done.11.refs_2_
  449.1 2.2 last_step.14.refs_3_
  451.3 2.2 last_step.15
  453.5 5.0 %maximum_convert_fusion = f32[8,6,64,512]{3,2,1,0:T(8,128)} fusion(bf16[4,6,64,512]{3,2,1,0:T(8,128)(2,1)} %bitcast.3, bf16[4,6,64,512]{3,2,1,0:T(8,128)(2,1)} %bitcast.2), kind=kLoop, calls=%fused_computation | loop fusion | flops 3145728 | bytes 9437184 | tf_op jit(solution)/shard_map/convert_element_type | solution.py:194
  (35 shorter events, 0.2 us)
Async XLA Ops:
  7.2 446.3 %reduce-scatter.3.cloned.1.call-start = ((), (), s32[]{:S(2)}) async-start(), calls=%async_computation.2 | async-start | bytes 14155776 | tf_op jit(solution)/shard_map/reduce_scatter | solution.py:147
  7.2 30.5 %copy-start.11 = (bf16[512,4096]{1,0:T(8,128)(2,1)S(1)}, bf16[512,4096]{1,0:T(8,128)(2,1)}, u32[]{:S(2)}) copy-start(bf16[512,4096]{1,0:T(8,128)(2,1)} %refs_3_.15) | copy-start | bytes 12582916
  8.7 29.0 %collective-permute-start.1 = (bf16[512,512]{1,0:T(8,128)(2,1)S(1)}, bf16[512,512]{1,0:T(8,128)(2,1)S(1)}, u32[]{:S(2)}, u32[]{:S(2)}) collective-permute-start(bf16[512,512]{1,0:T(8,128)(2,1)S(1)} %get-tuple-element.90), channel_id=1, source_target_pairs={{0,2},{1,3},{2,0},{3,1},{4,6},{5,7},{6,4},{7,5},{8,10},{9,11},{10,... | collective-permute-start | bytes 1572872 | tf_op jit(solution)/shard_map/ppermute | solution.py:32
  12.8 26.5 %collective-permute-start = (bf16[512,512]{1,0:T(8,128)(2,1)S(1)}, bf16[512,512]{1,0:T(8,128)(2,1)S(1)}, u32[]{:S(2)}, u32[]{:S(2)}) collective-permute-start(bf16[512,512]{1,0:T(8,128)(2,1)S(1)} %get-tuple-element.90), channel_id=1, source_target_pairs={{0,1},{1,0},{2,3},{3,2},{4,5},{5,4},{6,7},{7,6},{8,9},{9,8},{10,11... | collective-permute-start | bytes 1572872 | tf_op jit(solution)/shard_map/ppermute | solution.py:32
  15.6 97.8 %collective-permute-start.5 = (bf16[512,1024]{1,0:T(8,128)(2,1)S(1)}, bf16[512,1024]{1,0:T(8,128)(2,1)S(1)}, u32[]{:S(2)}, u32[]{:S(2)}) collective-permute-start(bf16[512,1024]{1,0:T(8,128)(2,1)S(1)} %slice.14), channel_id=1, source_target_pairs={{0,2},{1,3},{2,0},{3,1},{4,6},{5,7},{6,4},{7,5},{8,10},{9,11},{10,... | collective-permute-start | bytes 3145736 | tf_op jit(solution)/shard_map/ppermute | solution.py:32
  16.0 97.4 %collective-permute-start.4 = (bf16[512,1024]{1,0:T(8,128)(2,1)S(1)}, bf16[512,1024]{1,0:T(8,128)(2,1)S(1)}, u32[]{:S(2)}, u32[]{:S(2)}) collective-permute-start(bf16[512,1024]{1,0:T(8,128)(2,1)S(1)} %slice.14), channel_id=1, source_target_pairs={{0,1},{1,0},{2,3},{3,2},{4,5},{5,4},{6,7},{7,6},{8,9},{9,8},{10,11... | collective-permute-start | bytes 3145736 | tf_op jit(solution)/shard_map/ppermute | solution.py:32
  16.2 87.3 %collective-permute-start.7 = (bf16[512,512]{1,0:T(8,128)(2,1)S(1)}, bf16[512,512]{1,0:T(8,128)(2,1)S(1)}, u32[]{:S(2)}, u32[]{:S(2)}) collective-permute-start(bf16[512,512]{1,0:T(8,128)(2,1)S(1)} %get-tuple-element.89), channel_id=1, source_target_pairs={{0,2},{1,3},{2,0},{3,1},{4,6},{5,7},{6,4},{7,5},{8,10},{9,11},{10,... | collective-permute-start | bytes 1572872 | tf_op jit(solution)/shard_map/ppermute | solution.py:32
  37.7 66.0 %collective-permute-start.6 = (bf16[512,512]{1,0:T(8,128)(2,1)S(1)}, bf16[512,512]{1,0:T(8,128)(2,1)S(1)}, u32[]{:S(2)}, u32[]{:S(2)}) collective-permute-start(bf16[512,512]{1,0:T(8,128)(2,1)S(1)} %get-tuple-element.89), channel_id=1, source_target_pairs={{0,1},{1,0},{2,3},{3,2},{4,5},{5,4},{6,7},{7,6},{8,9},{9,8},{10,11... | collective-permute-start | bytes 1572872 | tf_op jit(solution)/shard_map/ppermute | solution.py:32
  48.1 64.5 %copy-start.1 = (bf16[512,512]{1,0:T(8,128)(2,1)}, bf16[512,512]{1,0:T(8,128)(2,1)S(1)}, u32[]{:S(2)}) copy-start(bf16[512,512]{1,0:T(8,128)(2,1)S(1)} %get-tuple-element.86) | copy-start | bytes 1572868
  48.1 64.5 %copy-start.3 = (bf16[512,512]{1,0:T(8,128)(2,1)}, bf16[512,512]{1,0:T(8,128)(2,1)S(1)}, u32[]{:S(2)}) copy-start(bf16[512,512]{1,0:T(8,128)(2,1)S(1)} %get-tuple-element.85) | copy-start | bytes 1572868
  112.6 0.8 copy-start.10
  113.4 9.2 %copy-start.7 = (bf16[512,512]{1,0:T(8,128)(2,1)}, bf16[512,512]{1,0:T(8,128)(2,1)S(1)}, u32[]{:S(2)}) copy-start(bf16[512,512]{1,0:T(8,128)(2,1)S(1)} %get-tuple-element.84) | copy-start | bytes 1572868
  122.6 0.8 copy-start.2
  132.4 0.8 copy-start.4
  133.2 0.8 copy-start.8
  134.1 319.4 %reduce-scatter.5.cloned.1.call-start = ((), (), s32[]{:S(2)}) async-start(), calls=%async_computation.3 | async-start | bytes 14155776 | tf_op jit(solution)/shard_map/reduce_scatter | solution.py:147
  134.1 92.9 %collective-permute-start.3 = (bf16[512,2048]{1,0:T(8,128)(2,1)}, bf16[512,2048]{1,0:T(8,128)(2,1)S(1)}, u32[]{:S(2)}, u32[]{:S(2)}) collective-permute-start(bf16[512,2048]{1,0:T(8,128)(2,1)} %slice.12), channel_id=1, source_target_pairs={{0,2},{1,3},{2,0},{3,1},{4,6},{5,7},{6,4},{7,5},{8,10},{9,11},{10,... | collective-permute-start | bytes 6291464 | tf_op jit(solution)/shard_map/ppermute | solution.py:32
  135.7 91.4 %collective-permute-start.2 = (bf16[512,2048]{1,0:T(8,128)(2,1)}, bf16[512,2048]{1,0:T(8,128)(2,1)S(1)}, u32[]{:S(2)}, u32[]{:S(2)}) collective-permute-start(bf16[512,2048]{1,0:T(8,128)(2,1)} %slice.12), channel_id=1, source_target_pairs={{0,1},{1,0},{2,3},{3,2},{4,5},{5,4},{6,7},{7,6},{8,9},{9,8},{10,11... | collective-permute-start | bytes 6291464 | tf_op jit(solution)/shard_map/ppermute | solution.py:32
  236.1 0.8 copy-start.6
  236.9 0.8 copy-start.9
  246.6 0.8 copy-start.5
  265.4 35.2 %collective-permute-start.20 = (bf16[512,512]{1,0:T(8,128)(2,1)}, bf16[512,512]{1,0:T(8,128)(2,1)S(1)}, u32[]{:S(2)}, u32[]{:S(2)}) collective-permute-start(bf16[512,512]{1,0:T(8,128)(2,1)} %copy-done.10), channel_id=1, source_target_pairs={{0,1},{1,0},{2,3},{3,2},{4,5},{5,4},{6,7},{7,6},{8,9},{9,8},{10,11... | collective-permute-start | bytes 1572872 | tf_op jit(solution)/shard_map/ppermute | solution.py:32
  265.8 34.8 %collective-permute-start.21 = (bf16[512,512]{1,0:T(8,128)(2,1)}, bf16[512,512]{1,0:T(8,128)(2,1)S(1)}, u32[]{:S(2)}, u32[]{:S(2)}) collective-permute-start(bf16[512,512]{1,0:T(8,128)(2,1)} %copy-done.7), channel_id=1, source_target_pairs={{0,2},{1,3},{2,0},{3,1},{4,6},{5,7},{6,4},{7,5},{8,10},{9,11},{10,... | collective-permute-start | bytes 1572872 | tf_op jit(solution)/shard_map/ppermute | solution.py:32
  269.2 46.7 %collective-permute-start.22 = (bf16[512,512]{1,0:T(8,128)(2,1)}, bf16[512,512]{1,0:T(8,128)(2,1)S(1)}, u32[]{:S(2)}, u32[]{:S(2)}) collective-permute-start(bf16[512,512]{1,0:T(8,128)(2,1)} %copy-done.3), channel_id=1, source_target_pairs={{0,1},{1,0},{2,3},{3,2},{4,5},{5,4},{6,7},{7,6},{8,9},{9,8},{10,11... | collective-permute-start | bytes 1572872 | tf_op jit(solution)/shard_map/ppermute | solution.py:32
  269.5 46.6 %collective-permute-start.23 = (bf16[512,512]{1,0:T(8,128)(2,1)}, bf16[512,512]{1,0:T(8,128)(2,1)S(1)}, u32[]{:S(2)}, u32[]{:S(2)}) collective-permute-start(bf16[512,512]{1,0:T(8,128)(2,1)} %copy-done.1), channel_id=1, source_target_pairs={{0,2},{1,3},{2,0},{3,1},{4,6},{5,7},{6,4},{7,5},{8,10},{9,11},{10,... | collective-permute-start | bytes 1572872 | tf_op jit(solution)/shard_map/ppermute | solution.py:32
  270.4 68.0 %collective-permute-start.16 = (bf16[512,512]{1,0:T(8,128)(2,1)}, bf16[512,512]{1,0:T(8,128)(2,1)S(1)}, u32[]{:S(2)}, u32[]{:S(2)}) collective-permute-start(bf16[512,512]{1,0:T(8,128)(2,1)} %copy-done.8), channel_id=1, source_target_pairs={{0,1},{1,0},{2,3},{3,2},{4,5},{5,4},{6,7},{7,6},{8,9},{9,8},{10,11... | collective-permute-start | bytes 1572872 | tf_op jit(solution)/shard_map/ppermute | solution.py:32
  300.6 38.0 %collective-permute-start.17 = (bf16[512,512]{1,0:T(8,128)(2,1)}, bf16[512,512]{1,0:T(8,128)(2,1)S(1)}, u32[]{:S(2)}, u32[]{:S(2)}) collective-permute-start(bf16[512,512]{1,0:T(8,128)(2,1)} %copy-done.4), channel_id=1, source_target_pairs={{0,2},{1,3},{2,0},{3,1},{4,6},{5,7},{6,4},{7,5},{8,10},{9,11},{10,... | collective-permute-start | bytes 1572872 | tf_op jit(solution)/shard_map/ppermute | solution.py:32
  300.6 60.2 %collective-permute-start.18 = (bf16[512,512]{1,0:T(8,128)(2,1)}, bf16[512,512]{1,0:T(8,128)(2,1)S(1)}, u32[]{:S(2)}, u32[]{:S(2)}) collective-permute-start(bf16[512,512]{1,0:T(8,128)(2,1)} %copy-done.2), channel_id=1, source_target_pairs={{0,1},{1,0},{2,3},{3,2},{4,5},{5,4},{6,7},{7,6},{8,9},{9,8},{10,11... | collective-permute-start | bytes 1572872 | tf_op jit(solution)/shard_map/ppermute | solution.py:32
  315.9 45.3 %collective-permute-start.19 = (bf16[512,512]{1,0:T(8,128)(2,1)S(1)}, bf16[512,512]{1,0:T(8,128)(2,1)S(1)}, u32[]{:S(2)}, u32[]{:S(2)}) collective-permute-start(bf16[512,512]{1,0:T(8,128)(2,1)S(1)} %get-tuple-element.82), channel_id=1, source_target_pairs={{0,2},{1,3},{2,0},{3,1},{4,6},{5,7},{6,4},{7,5},{8,10},{9,11},{10,... | collective-permute-start | bytes 1572872 | tf_op jit(solution)/shard_map/ppermute | solution.py:32
  316.1 67.1 %collective-permute-start.14 = (bf16[512,512]{1,0:T(8,128)(2,1)}, bf16[512,512]{1,0:T(8,128)(2,1)S(1)}, u32[]{:S(2)}, u32[]{:S(2)}) collective-permute-start(bf16[512,512]{1,0:T(8,128)(2,1)} %copy-done.9), channel_id=1, source_target_pairs={{0,1},{1,0},{2,3},{3,2},{4,5},{5,4},{6,7},{7,6},{8,9},{9,8},{10,11... | collective-permute-start | bytes 1572872 | tf_op jit(solution)/shard_map/ppermute | solution.py:32
  338.4 45.3 %collective-permute-start.15 = (bf16[512,512]{1,0:T(8,128)(2,1)}, bf16[512,512]{1,0:T(8,128)(2,1)S(1)}, u32[]{:S(2)}, u32[]{:S(2)}) collective-permute-start(bf16[512,512]{1,0:T(8,128)(2,1)} %copy-done.6), channel_id=1, source_target_pairs={{0,2},{1,3},{2,0},{3,1},{4,6},{5,7},{6,4},{7,5},{8,10},{9,11},{10,... | collective-permute-start | bytes 1572872 | tf_op jit(solution)/shard_map/ppermute | solution.py:32
  338.6 67.0 %collective-permute-start.12 = (bf16[512,512]{1,0:T(8,128)(2,1)}, bf16[512,512]{1,0:T(8,128)(2,1)S(1)}, u32[]{:S(2)}, u32[]{:S(2)}) collective-permute-start(bf16[512,512]{1,0:T(8,128)(2,1)} %copy-done.5), channel_id=1, source_target_pairs={{0,1},{1,0},{2,3},{3,2},{4,5},{5,4},{6,7},{7,6},{8,9},{9,8},{10,11... | collective-permute-start | bytes 1572872 | tf_op jit(solution)/shard_map/ppermute | solution.py:32
  360.8 73.0 %collective-permute-start.13 = (bf16[512,512]{1,0:T(8,128)(2,1)S(1)}, bf16[512,512]{1,0:T(8,128)(2,1)S(1)}, u32[]{:S(2)}, u32[]{:S(2)}) collective-permute-start(bf16[512,512]{1,0:T(8,128)(2,1)S(1)} %get-tuple-element.76), channel_id=1, source_target_pairs={{0,2},{1,3},{2,0},{3,1},{4,6},{5,7},{6,4},{7,5},{8,10},{9,11},{10,... | collective-permute-start | bytes 1572872 | tf_op jit(solution)/shard_map/ppermute | solution.py:32
  361.2 90.1 %collective-permute-start.8 = (bf16[512,512]{1,0:T(8,128)(2,1)S(1)}, bf16[512,512]{1,0:T(8,128)(2,1)S(1)}, u32[]{:S(2)}, u32[]{:S(2)}) collective-permute-start(bf16[512,512]{1,0:T(8,128)(2,1)S(1)} %get-tuple-element.71), channel_id=1, source_target_pairs={{0,1},{1,0},{2,3},{3,2},{4,5},{5,4},{6,7},{7,6},{8,9},{9,8},{10,11... | collective-permute-start | bytes 1572872 | tf_op jit(solution)/shard_map/ppermute | solution.py:32
  383.2 68.1 %collective-permute-start.9 = (bf16[512,512]{1,0:T(8,128)(2,1)S(1)}, bf16[512,512]{1,0:T(8,128)(2,1)S(1)}, u32[]{:S(2)}, u32[]{:S(2)}) collective-permute-start(bf16[512,512]{1,0:T(8,128)(2,1)S(1)} %get-tuple-element.72), channel_id=1, source_target_pairs={{0,2},{1,3},{2,0},{3,1},{4,6},{5,7},{6,4},{7,5},{8,10},{9,11},{10,... | collective-permute-start | bytes 1572872 | tf_op jit(solution)/shard_map/ppermute | solution.py:32
  383.7 62.4 %collective-permute-start.10 = (bf16[512,512]{1,0:T(8,128)(2,1)S(1)}, bf16[512,512]{1,0:T(8,128)(2,1)S(1)}, u32[]{:S(2)}, u32[]{:S(2)}) collective-permute-start(bf16[512,512]{1,0:T(8,128)(2,1)S(1)} %get-tuple-element.73), channel_id=1, source_target_pairs={{0,1},{1,0},{2,3},{3,2},{4,5},{5,4},{6,7},{7,6},{8,9},{9,8},{10,11... | collective-permute-start | bytes 1572872 | tf_op jit(solution)/shard_map/ppermute | solution.py:32
  405.7 43.5 %collective-permute-start.11 = (bf16[512,512]{1,0:T(8,128)(2,1)S(1)}, bf16[512,512]{1,0:T(8,128)(2,1)S(1)}, u32[]{:S(2)}, u32[]{:S(2)}) collective-permute-start(bf16[512,512]{1,0:T(8,128)(2,1)S(1)} %get-tuple-element.74), channel_id=1, source_target_pairs={{0,2},{1,3},{2,0},{3,1},{4,6},{5,7},{6,4},{7,5},{8,10},{9,11},{10,... | collective-permute-start | bytes 1572872 | tf_op jit(solution)/shard_map/ppermute | solution.py:32
  405.7 2.2 copy-start
Sparse Core Ops, SparseCore 0:
  134.2 93.3 reduce-scatter.2
  265.5 93.2 reduce-scatter.4

commit v2 on v1

--- a/solution.py
+++ b/solution.py
@@ -8,6 +8,9 @@
 from jax.sharding import PartitionSpec as P
 
 VMEM_BYTES = 48 * 2**20
+LAG = 6
+WINDOW = 2
+TIE = 1
 GELU_SCALE = 0.7978845608028654
 GELU_CUBIC = 0.044715
 
@@ -80,71 +83,88 @@
     def column(index):
         return pl.BlockSpec((rows, width), lambda *_: (0, index))
 
-    groups, first = [], 0
-    while first < blocks:
-        size = max(first, 1)
-        groups.append((first, size))
-        first += size
-
-    arrived = []
-    for index, (first, size) in enumerate(groups):
-        piece = tokens[:, first * width : (first + size) * width]
-        if index >= 3:
-            piece, arrived[index - 3] = lax.optimization_barrier((piece, arrived[index - 3]))
-        arrived.append([swapped(piece, level) for level in reversed(range(far))][::-1])
+    order = []
+    for block in range(blocks):
+        order.append((False, block))
+        if block >= LAG:
+            order.append((True, block - LAG))
+    order += [(True, block) for block in range(max(blocks - LAG, 0), blocks)]
 
     halves = 2 if blocks > 1 else 1
     per_half = blocks // halves
-    output = delta = None
-    received, scattered = [], []
-    for (first, size), pieces in zip(groups, arrived):
-        for block in range(first, first + size):
-            if block % per_half == 0:
-                grads = None
-            at = block % per_half
-            parts = [tokens] + [tokens] * (near - 1) + list(pieces)
-            specs = [column(block)] + [column(block ^ (1 << bit)) for bit in range(near - 1)]
-            specs += [column(block - first)] * far
-            operands = parts + [weight, cotangent]
-            specs += [
-                pl.BlockSpec((1, partners, width, width), lambda *_, block=block: (block, 0, 0, 0)),
+    output = delta = grads = None
+    ahead, back, terms, scattered, landed = {}, {}, {}, [], []
+
+    def step(block):
+        nonlocal output, delta, grads
+        pieces = ahead[block]
+        if block >= LAG:
+            pieces, back[block - LAG] = lax.optimization_barrier((pieces, back[block - LAG]))
+        at = block % per_half
+        if at == 0:
+            grads = None
+        operands = [tokens] * near + pieces + [weight, cotangent]
+        specs = [column(block)] + [column(block ^ (1 << bit)) for bit in range(near - 1)]
+        specs += [column(0)] * far
+        specs += [pl.BlockSpec((1, partners, width, width), lambda *_: (block, 0, 0, 0)), column(block)]
+        aliases = {}
+        for where, chained in enumerate((output, delta, grads)):
+            if chained is not None:
+                aliases[len(operands)] = where
+                operands.append(chained)
+                specs.append(any_spec)
+        moved = 2 * (3 * partners * width * width + rows * width * (partners + far + 3))
+        output, delta, grads, *terms[block] = pl.pallas_call(
+            partial(block_step, partners, near, split),
+            grid=(1,),
+            in_specs=specs,
+            out_specs=[
                 column(block),
+                column(block),
+                pl.BlockSpec((split, 1, partners, shard, width), lambda *_: (0, at, 0, 0, 0)),
             ]
-            aliases = {}
-            for where, chained in enumerate((output, delta, grads)):
-                if chained is not None:
-                    aliases[len(operands)] = where
-                    operands.append(chained)
-                    specs.append(any_spec)
-            moved = 2 * (3 * partners * width * width + rows * width * (partners + far + 3))
-            output, delta, grads, *terms = pl.pallas_call(
-                partial(block_step, partners, near, split),
-                grid=(1,),
-                in_specs=specs,
-                out_specs=[
-                    column(block),
-                    column(block),
-                    pl.BlockSpec((split, 1, partners, shard, width), lambda *_, at=at: (0, at, 0, 0, 0)),
-                ]
-                + [column(0)] * far,
-                out_shape=[
-                    jax.ShapeDtypeStruct(tokens.shape, sixteen),
-                    jax.ShapeDtypeStruct(tokens.shape, sixteen),
-                    jax.ShapeDtypeStruct((split, per_half, partners, shard, width), sixteen),
-                ]
-                + [jax.ShapeDtypeStruct((rows, width), sixteen)] * far,
-                input_output_aliases=aliases,
-                compiler_params=params,
-                cost_estimate=pl.CostEstimate(
-                    flops=2 * rows * width * width * (2 * partners + far),
-                    bytes_accessed=moved,
-                    transcendentals=rows * width,
-                ),
-                name="block_step",
-            )(*operands)
-            received.append([swapped(terms[level], level) for level in reversed(range(far))][::-1])
-            if at == per_half - 1:
+            + [column(0)] * far,
+            out_shape=[
+                jax.ShapeDtypeStruct(tokens.shape, sixteen),
+                jax.ShapeDtypeStruct(tokens.shape, sixteen),
+                jax.ShapeDtypeStruct((split, per_half, partners, shard, width), sixteen),
+            ]
+            + [jax.ShapeDtypeStruct((rows, width), sixteen)] * far,
+            input_output_aliases=aliases,
+            compiler_params=params,
+            cost_estimate=pl.CostEstimate(
+                flops=2 * rows * width * width * (2 * partners + far),
+                bytes_accessed=moved,
+                transcendentals=rows * width,
+            ),
+            name="block_step",
+        )(*operands)
+        if at == per_half - 1:
+            if TIE:
+                waiting.append([order.index((False, block)) + TIE, grads])
+            else:
                 scattered.append(lax.psum_scatter(grads, "dp", scatter_dimension=0, tiled=False))
+
+    waiting = []
+    for place, (backward, block) in enumerate(order):
+        if backward:
+            step(block)
+            pieces = terms[block]
+        else:
+            pieces = [tokens[:, block * width : (block + 1) * width]] * far
+        if place >= WINDOW:
+            was, before = order[place - WINDOW]
+            held = (back if was else ahead)[before]
+            pieces, held = lax.optimization_barrier((pieces, held))
+            (back if was else ahead)[before] = held
+        sent = [swapped(pieces[level], level) for level in reversed(range(far))][::-1]
+        (back if backward else ahead)[block] = sent
+    for place, grads in waiting:
+        was, before = order[place]
+        held = (back if was else ahead)[before]
+        grads, held = lax.optimization_barrier((grads, held))
+        (back if was else ahead)[before] = held
+        scattered.append(lax.psum_scatter(grads, "dp", scatter_dimension=0, tiled=False))
 
     near_total = pl.pallas_call(
         partial(near_step, near),
@@ -168,9 +188,12 @@
         name="near_step",
     )(*[delta] * near, *[weight] * near)
 
+    weight_grad = jnp.concatenate(scattered, axis=0).astype(jnp.float32)
     input_grad = None
     for block in range(blocks):
-        operands = [near_total] + received[block]
+        if block == max(blocks - 2, 0):
+            weight_grad, back[block] = lax.optimization_barrier((weight_grad, back[block]))
+        operands = [near_total] + back[block]
         specs = [column(block)] + [column(0)] * far
         aliases = {}
         if input_grad is not None:
@@ -191,7 +214,6 @@
             name="last_step",
         )(*operands)
 
-    weight_grad = jnp.concatenate(scattered, axis=0).astype(jnp.float32)
     return output, input_grad, weight_grad
 
 

time: 466 us -> 402 us (0.86)
  waiting for transfers between devices: 306 us -> 229 us
  starting transfers between devices: 24.2 us -> 38.7 us
    ppermute x24 -> x32, waiting for transfers between devices: 306 us -> 229 us  [swapped(): return lax.ppermute(value, 'feat', pairs)]
    ppermute x24 -> x32, starting transfers between devices: 24.1 us -> 38.6 us  [swapped(): return lax.ppermute(value, 'feat', pairs)]
  transfers between devices with their start and end apart: 26 -> 34, of which waited for: 17 -> 24; matrix products, arithmetic and copies ran while one was open for 1% -> 1% of each run, Pallas kernels for 18% -> 26%
where the time goes in v2:
time: 402 us; the launch traced here: 401 us
  waiting for transfers between devices  229 us (57%)
  Pallas kernels  105 us (26%)
  starting transfers between devices  38.7 us (10%)
  between operations  14.2 us (4%)
  local copies, waits for them, and re-layouts  8.95 us (2%)
  other arithmetic  4.99 us (1%)
    ppermute x32, waiting for transfers between devices, swapped(): return lax.ppermute(value, 'feat', pairs)  229 us
    pallas_call x8, Pallas kernels, step(): pl.pallas_call(partial(block_step, partners, near, split), grid=(1,), in_...  72.4 us
    ppermute x32, starting transfers between devices, swapped(): return lax.ppermute(value, 'feat', pairs)  38.6 us
    pallas_call x8, Pallas kernels, local(): pl.pallas_call(partial(last_step, far), grid=(1,), in_specs=specs, out_sp...  17.4 us
    pallas_call x1, Pallas kernels, local(): pl.pallas_call(partial(near_step, near), grid=(blocks,), in_specs=[pl.Blo...  15.2 us
  transfers between devices with their start and end apart: 34, of which 24 were waited for; matrix products, arithmetic and copies ran while one was open for 1% of the time, Pallas kernels for 26%

profile of v2, /device:TPU:0, one launch (start us, length us, event | category | flops | bytes accessed | tf_op | source)
XLA Modules:
  0.0 401.0 jit_solution(11949498380296907415)
XLA Ops:
  7.2 3.5 fusion
  10.7 4.0 %collective-permute-start.5 = (bf16[512,512]{1,0:T(8,128)(2,1)S(1)}, bf16[512,512]{1,0:T(8,128)(2,1)S(1)}, u32[]{:S(2)}, u32[]{:S(2)}) collective-permute-start(bf16[512,512]{1,0:T(8,128)(2,1)S(1)} %get-tuple-element.228), channel_id=1, source_target_pairs={{0,2},{1,3},{2,0},{3,1},{4,6},{5,7},{6,4},{7,5},{8,10},{9,11},{10,... | collective-permute-start | bytes 1572872 | tf_op jit(solution)/shard_map/ppermute | solution.py:35
  14.8 1.6 collective-permute-start.4
  16.8 22.9 %collective-permute-done.5.refs_5_ = bf16[512,512]{1,0:T(8,128)(2,1)S(1)} collective-permute-done((bf16[512,512]{1,0:T(8,128)(2,1)S(1)}, bf16[512,512]{1,0:T(8,128)(2,1)S(1)}, u32[]{:S(2)}, u32[]{:S(2)}) %collective-permute-start.5) | collective-permute-done | bytes 524320 | tf_op jit(solution)/shard_map/ppermute | solution.py:35
  39.7 1.2 collective-permute-done.4.refs_4_
  40.9 2.5 collective-permute-start.13
  43.3 18.0 %collective-permute-done.1.refs_5_ = bf16[512,512]{1,0:T(8,128)(2,1)S(1)} collective-permute-done((bf16[512,512]{1,0:T(8,128)(2,1)S(1)}, bf16[512,512]{1,0:T(8,128)(2,1)S(1)}, u32[]{:S(2)}, u32[]{:S(2)}) %collective-permute-start.1) | collective-permute-done | bytes 524320 | tf_op jit(solution)/shard_map/ppermute | solution.py:35
  61.4 13.2 %collective-permute-done.refs_4_ = bf16[512,512]{1,0:T(8,128)(2,1)S(1)} collective-permute-done((bf16[512,512]{1,0:T(8,128)(2,1)S(1)}, bf16[512,512]{1,0:T(8,128)(2,1)S(1)}, u32[]{:S(2)}, u32[]{:S(2)}) %collective-permute-start) | collective-permute-done | bytes 524320 | tf_op jit(solution)/shard_map/ppermute | solution.py:35
  74.6 1.3 collective-permute-start.3
  75.9 8.9 %block_step.8 = (bf16[512,4096]{1,0:T(8,128)(2,1)}, bf16[512,4096]{1,0:T(8,128)(2,1)}, bf16[8,4,6,64,512]{4,3,2,1,0:T(8,128)(2,1)}, bf16[512,512]{1,0:T(8,128)(2,1)S(1)}, bf16[512,512]{1,0:T(8,128)(2,1)S(1)}) custom-call(bf16[512,4096]{1,0:T(8,128)(2,1)} %refs_3_.15, bf16[512,4096]{1,0:T(8,128)(2,1)} %refs_3_.15, bf16[512,4096]{1,0:T(8,128)(2,1)} %refs_3_.15, ...), custom_call_target="tpu_custom_call" | custom-call | flops 3758096384 | bytes 15204352 | tf_op jit(solution)/shard_map/block_step/pallas_call | solution.py:117
  84.8 0.8 copy-done.15
  85.6 9.1 %block_step.9 = (bf16[512,4096]{1,0:T(8,128)(2,1)}, bf16[512,4096]{1,0:T(8,128)(2,1)}, bf16[8,4,6,64,512]{4,3,2,1,0:T(8,128)(2,1)}, bf16[512,512]{1,0:T(8,128)(2,1)S(1)}, bf16[512,512]{1,0:T(8,128)(2,1)S(1)}) custom-call(bf16[512,4096]{1,0:T(8,128)(2,1)} %refs_3_.15, ...), custom_call_target="tpu_custom_call", output_to_operand_aliasing={{0}: (8, {}), {1}: (9, {}), {2}: (10, {})} | custom-call | flops 3758096384 | bytes 15204352 | tf_op jit(solution)/shard_map/block_step/pallas_call | solution.py:117
  94.7 11.0 %collective-permute-done.2.refs_4_ = bf16[512,512]{1,0:T(8,128)(2,1)S(1)} collective-permute-done((bf16[512,512]{1,0:T(8,128)(2,1)S(1)}, bf16[512,512]{1,0:T(8,128)(2,1)S(1)}, u32[]{:S(2)}, u32[]{:S(2)}) %collective-permute-start.2) | collective-permute-done | bytes 524320 | tf_op jit(solution)/shard_map/ppermute | solution.py:35
  105.6 1.5 collective-permute-start.6
  107.1 1.6 collective-permute-start.7
  108.7 8.9 %block_step.10 = (bf16[512,4096]{1,0:T(8,128)(2,1)}, bf16[512,4096]{1,0:T(8,128)(2,1)}, bf16[8,4,6,64,512]{4,3,2,1,0:T(8,128)(2,1)}, bf16[512,512]{1,0:T(8,128)(2,1)S(1)}, bf16[512,512]{1,0:T(8,128)(2,1)S(1)}) custom-call(bf16[512,4096]{1,0:T(8,128)(2,1)} %refs_3_.15, ...), custom_call_target="tpu_custom_call", output_to_operand_aliasing={{0}: (8, {}), {1}: (9, {}), {2}: (10, {})} | custom-call | flops 3758096384 | bytes 15204352 | tf_op jit(solution)/shard_map/block_step/pallas_call | solution.py:117
  117.7 9.1 %block_step.11 = (bf16[512,4096]{1,0:T(8,128)(2,1)}, bf16[512,4096]{1,0:T(8,128)(2,1)}, bf16[8,4,6,64,512]{4,3,2,1,0:T(8,128)(2,1)}, bf16[512,512]{1,0:T(8,128)(2,1)S(1)}, bf16[512,512]{1,0:T(8,128)(2,1)S(1)}) custom-call(bf16[512,4096]{1,0:T(8,128)(2,1)} %refs_3_.15, ...), custom_call_target="tpu_custom_call", output_to_operand_aliasing={{0}: (8, {}), {1}: (9, {}), {2}: (10, {})} | custom-call | flops 3758096384 | bytes 15204352 | tf_op jit(solution)/shard_map/block_step/pallas_call | solution.py:117
  126.8 2.4 collective-permute-done.6.refs_4_
  129.3 2.7 collective-permute-done.7.refs_5_
  132.4 2.7 collective-permute-start.15
  135.2 1.9 collective-permute-start.9
  137.0 25.7 %collective-permute-done.14.refs_4_ = bf16[512,512]{1,0:T(8,128)(2,1)S(1)} collective-permute-done((bf16[512,512]{1,0:T(8,128)(2,1)}, bf16[512,512]{1,0:T(8,128)(2,1)S(1)}, u32[]{:S(2)}, u32[]{:S(2)}) %collective-permute-start.14) | collective-permute-done | bytes 524320 | tf_op jit(solution)/shard_map/ppermute | solution.py:35
  162.8 3.6 collective-permute-start.17
  166.4 9.1 %block_step.12 = (bf16[512,4096]{1,0:T(8,128)(2,1)}, bf16[512,4096]{1,0:T(8,128)(2,1)}, bf16[8,4,6,64,512]{4,3,2,1,0:T(8,128)(2,1)}, bf16[512,512]{1,0:T(8,128)(2,1)S(1)}, bf16[512,512]{1,0:T(8,128)(2,1)S(1)}) custom-call(bf16[512,4096]{1,0:T(8,128)(2,1)} %refs_3_.15, bf16[512,4096]{1,0:T(8,128)(2,1)} %refs_3_.15, ...), custom_call_target="tpu_custom_call", output_to_operand_aliasing={{0}: (8, {}), {1}: (9, {})} | custom-call | flops 3758096384 | bytes 15204352 | tf_op jit(solution)/shard_map/block_step/pallas_call | solution.py:117
  175.5 0.8 copy-done.14
  176.3 5.2 %collective-permute-done.8.refs_4_ = bf16[512,512]{1,0:T(8,128)(2,1)S(1)} collective-permute-done((bf16[512,512]{1,0:T(8,128)(2,1)}, bf16[512,512]{1,0:T(8,128)(2,1)S(1)}, u32[]{:S(2)}, u32[]{:S(2)}) %collective-permute-start.8) | collective-permute-done | bytes 524320 | tf_op jit(solution)/shard_map/ppermute | solution.py:35
  181.5 0.8 collective-permute-done.9.refs_5_
  182.2 2.8 collective-permute-start.11
  185.0 18.9 %collective-permute-done.16.refs_1_ = bf16[512,512]{1,0:T(8,128)(2,1)S(1)} collective-permute-done((bf16[512,512]{1,0:T(8,128)(2,1)}, bf16[512,512]{1,0:T(8,128)(2,1)S(1)}, u32[]{:S(2)}, u32[]{:S(2)}) %collective-permute-start.16) | collective-permute-done | bytes 524320 | tf_op jit(solution)/shard_map/ppermute | solution.py:35
  203.9 0.8 collective-permute-done.17.refs_2_
  204.7 2.8 collective-permute-start.19
  207.5 8.8 %block_step.13 = (bf16[512,4096]{1,0:T(8,128)(2,1)}, bf16[512,4096]{1,0:T(8,128)(2,1)}, bf16[8,4,6,64,512]{4,3,2,1,0:T(8,128)(2,1)}, bf16[512,512]{1,0:T(8,128)(2,1)S(1)}, bf16[512,512]{1,0:T(8,128)(2,1)S(1)}) custom-call(bf16[512,4096]{1,0:T(8,128)(2,1)} %refs_3_.15, ...), custom_call_target="tpu_custom_call", output_to_operand_aliasing={{0}: (8, {}), {1}: (9, {}), {2}: (10, {})} | custom-call | flops 3758096384 | bytes 15204352 | tf_op jit(solution)/shard_map/block_step/pallas_call | solution.py:117
  216.3 9.3 %block_step.14 = (bf16[512,4096]{1,0:T(8,128)(2,1)}, bf16[512,4096]{1,0:T(8,128)(2,1)}, bf16[8,4,6,64,512]{4,3,2,1,0:T(8,128)(2,1)}, bf16[512,512]{1,0:T(8,128)(2,1)S(1)}, bf16[512,512]{1,0:T(8,128)(2,1)S(1)}) custom-call(bf16[512,4096]{1,0:T(8,128)(2,1)} %refs_3_.15, ...), custom_call_target="tpu_custom_call", output_to_operand_aliasing={{0}: (8, {}), {1}: (9, {}), {2}: (10, {})} | custom-call | flops 3758096384 | bytes 15204352 | tf_op jit(solution)/shard_map/block_step/pallas_call | solution.py:117
  225.6 0.7 collective-permute-done.10.refs_4_
  226.4 0.9 collective-permute-done.11.refs_5_
  227.2 15.6 %collective-permute-done.18.refs_1_ = bf16[512,512]{1,0:T(8,128)(2,1)S(1)} collective-permute-done((bf16[512,512]{1,0:T(8,128)(2,1)S(1)}, bf16[512,512]{1,0:T(8,128)(2,1)S(1)}, u32[]{:S(2)}, u32[]{:S(2)}) %collective-permute-start.18) | collective-permute-done | bytes 524320 | tf_op jit(solution)/shard_map/ppermute | solution.py:35
  242.8 3.6 collective-permute-done.19.refs_2_
  246.4 9.1 %block_step.15 = (bf16[512,4096]{1,0:T(8,128)(2,1)}, bf16[512,4096]{1,0:T(8,128)(2,1)}, bf16[8,4,6,64,512]{4,3,2,1,0:T(8,128)(2,1)}, bf16[512,512]{1,0:T(8,128)(2,1)S(1)}, bf16[512,512]{1,0:T(8,128)(2,1)S(1)}) custom-call(bf16[512,4096]{1,0:T(8,128)(2,1)} %refs_3_.15, ...), custom_call_target="tpu_custom_call", output_to_operand_aliasing={{0}: (8, {}), {1}: (9, {}), {2}: (10, {})} | custom-call | flops 3758096384 | bytes 15204352 | tf_op jit(solution)/shard_map/block_step/pallas_call | solution.py:117
  255.5 0.8 copy-done.11
  256.3 0.8 copy-done.13
  257.2 2.0 collective-permute-start.27
  259.5 2.6 collective-permute-start.21
  262.1 24.5 %collective-permute-done.26.refs_1_ = bf16[512,512]{1,0:T(8,128)(2,1)S(1)} collective-permute-done((bf16[512,512]{1,0:T(8,128)(2,1)S(1)}, bf16[512,512]{1,0:T(8,128)(2,1)S(1)}, u32[]{:S(2)}, u32[]{:S(2)}) %collective-permute-start.26) | collective-permute-done | bytes 524320 | tf_op jit(solution)/shard_map/ppermute | solution.py:35
  286.7 19.0 %collective-permute-done.20.refs_1_ = bf16[512,512]{1,0:T(8,128)(2,1)S(1)} collective-permute-done((bf16[512,512]{1,0:T(8,128)(2,1)S(1)}, bf16[512,512]{1,0:T(8,128)(2,1)S(1)}, u32[]{:S(2)}, u32[]{:S(2)}) %collective-permute-start.20) | collective-permute-done | bytes 524320 | tf_op jit(solution)/shard_map/ppermute | solution.py:35
  305.7 1.2 collective-permute-done.21.refs_2_
  306.9 2.2 collective-permute-start.23
  309.1 19.1 %collective-permute-done.28.refs_1_ = bf16[512,512]{1,0:T(8,128)(2,1)S(1)} collective-permute-done((bf16[512,512]{1,0:T(8,128)(2,1)}, bf16[512,512]{1,0:T(8,128)(2,1)S(1)}, u32[]{:S(2)}, u32[]{:S(2)}) %collective-permute-start.28) | collective-permute-done | bytes 524320 | tf_op jit(solution)/shard_map/ppermute | solution.py:35
  328.2 1.2 collective-permute-done.29.refs_2_
  329.4 2.1 collective-permute-start.31
  331.5 19.1 %collective-permute-done.22.refs_1_ = bf16[512,512]{1,0:T(8,128)(2,1)S(1)} collective-permute-done((bf16[512,512]{1,0:T(8,128)(2,1)}, bf16[512,512]{1,0:T(8,128)(2,1)S(1)}, u32[]{:S(2)}, u32[]{:S(2)}) %collective-permute-start.22) | collective-permute-done | bytes 524320 | tf_op jit(solution)/shard_map/ppermute | solution.py:35
  350.6 1.3 collective-permute-done.23.refs_2_
  351.9 2.1 collective-permute-start.25
  354.0 2.2 copy-done
  356.2 15.2 %near_step.1.refs_0_ = f32[512,4096]{1,0:T(8,128)} custom-call(bf16[512,4096]{1,0:T(8,128)(2,1)S(1)} %copy-done, bf16[512,4096]{1,0:T(8,128)(2,1)S(1)} %copy-done, bf16[512,4096]{1,0:T(8,128)(2,1)S(1)} %copy-done, bf16[512,4096]{1,0:T(8,128)(2,1)S(1)} %copy-done, bf16[8,6,512,512]{3,2,1,0:T(8,128)(2,1)} %refs_7_.17, bf16[8,6,512,512]{3,2,1,0:T(8,128)(2,1)} %refs_7_.17, ...), custom_call_target="tpu_custom_call" | custom-call | flops 8589934592 | bytes 41943040 | tf_op jit(solution)/shard_map/near_step/pallas_call | solution.py:169
  371.4 2.2 last_step.8.refs_3_
  373.6 2.2 last_step.9.refs_3_
  375.8 2.2 last_step.10.refs_3_
  377.9 2.2 last_step.11.refs_3_
  380.1 2.2 last_step.12.refs_3_
  382.3 2.2 last_step.13.refs_3_
  384.5 5.0 %maximum_convert_fusion = f32[8,6,64,512]{3,2,1,0:T(8,128)} fusion(bf16[4,6,64,512]{3,2,1,0:T(8,128)(2,1)} %bitcast.3, bf16[4,6,64,512]{3,2,1,0:T(8,128)(2,1)} %bitcast.2), kind=kLoop, calls=%fused_computation | loop fusion | flops 3145728 | bytes 9437184 | tf_op jit(solution)/shard_map/convert_element_type | solution.py:191
  389.5 2.2 last_step.14.refs_3_
  391.6 0.4 collective-permute-done.25.refs_2_
  392.0 2.2 last_step.15
  (65 shorter events, 1.5 us)
Async XLA Ops:
  7.2 377.3 %reduce-scatter.3.cloned.1.call-start = ((), (), s32[]{:S(2)}) async-start(), calls=%async_computation.2 | async-start | bytes 14155776 | tf_op jit(solution)/shard_map/reduce_scatter | solution.py:167
  10.7 28.9 %collective-permute-start.5 = (bf16[512,512]{1,0:T(8,128)(2,1)S(1)}, bf16[512,512]{1,0:T(8,128)(2,1)S(1)}, u32[]{:S(2)}, u32[]{:S(2)}) collective-permute-start(bf16[512,512]{1,0:T(8,128)(2,1)S(1)} %get-tuple-element.228), channel_id=1, source_target_pairs={{0,2},{1,3},{2,0},{3,1},{4,6},{5,7},{6,4},{7,5},{8,10},{9,11},{10,... | collective-permute-start | bytes 1572872 | tf_op jit(solution)/shard_map/ppermute | solution.py:35
  14.8 26.1 %collective-permute-start.4 = (bf16[512,512]{1,0:T(8,128)(2,1)S(1)}, bf16[512,512]{1,0:T(8,128)(2,1)S(1)}, u32[]{:S(2)}, u32[]{:S(2)}) collective-permute-start(bf16[512,512]{1,0:T(8,128)(2,1)S(1)} %get-tuple-element.228), channel_id=1, source_target_pairs={{0,1},{1,0},{2,3},{3,2},{4,5},{5,4},{6,7},{7,6},{8,9},{9,8},{10,11... | collective-permute-start | bytes 1572872 | tf_op jit(solution)/shard_map/ppermute | solution.py:35
  16.4 45.0 %collective-permute-start.1 = (bf16[512,512]{1,0:T(8,128)(2,1)S(1)}, bf16[512,512]{1,0:T(8,128)(2,1)S(1)}, u32[]{:S(2)}, u32[]{:S(2)}) collective-permute-start(bf16[512,512]{1,0:T(8,128)(2,1)S(1)} %get-tuple-element.230), channel_id=1, source_target_pairs={{0,2},{1,3},{2,0},{3,1},{4,6},{5,7},{6,4},{7,5},{8,10},{9,11},{10,... | collective-permute-start | bytes 1572872 | tf_op jit(solution)/shard_map/ppermute | solution.py:35
  16.7 57.9 %collective-permute-start = (bf16[512,512]{1,0:T(8,128)(2,1)S(1)}, bf16[512,512]{1,0:T(8,128)(2,1)S(1)}, u32[]{:S(2)}, u32[]{:S(2)}) collective-permute-start(bf16[512,512]{1,0:T(8,128)(2,1)S(1)} %get-tuple-element.230), channel_id=1, source_target_pairs={{0,1},{1,0},{2,3},{3,2},{4,5},{5,4},{6,7},{7,6},{8,9},{9,8},{10,11... | collective-permute-start | bytes 1572872 | tf_op jit(solution)/shard_map/ppermute | solution.py:35
  40.9 76.8 %collective-permute-start.12 = (bf16[512,512]{1,0:T(8,128)(2,1)S(1)}, bf16[512,512]{1,0:T(8,128)(2,1)S(1)}, u32[]{:S(2)}, u32[]{:S(2)}) collective-permute-start(bf16[512,512]{1,0:T(8,128)(2,1)S(1)} %get-tuple-element.139), channel_id=1, source_target_pairs={{0,1},{1,0},{2,3},{3,2},{4,5},{5,4},{6,7},{7,6},{8,9},{9,8},{10,11... | collective-permute-start | bytes 1572872 | tf_op jit(solution)/shard_map/ppermute | solution.py:35
  40.9 76.8 %collective-permute-start.13 = (bf16[512,512]{1,0:T(8,128)(2,1)S(1)}, bf16[512,512]{1,0:T(8,128)(2,1)S(1)}, u32[]{:S(2)}, u32[]{:S(2)}) collective-permute-start(bf16[512,512]{1,0:T(8,128)(2,1)S(1)} %get-tuple-element.139), channel_id=1, source_target_pairs={{0,2},{1,3},{2,0},{3,1},{4,6},{5,7},{6,4},{7,5},{8,10},{9,11},{10,... | collective-permute-start | bytes 1572872 | tf_op jit(solution)/shard_map/ppermute | solution.py:35
  74.6 31.1 %collective-permute-start.2 = (bf16[512,512]{1,0:T(8,128)(2,1)S(1)}, bf16[512,512]{1,0:T(8,128)(2,1)S(1)}, u32[]{:S(2)}, u32[]{:S(2)}) collective-permute-start(bf16[512,512]{1,0:T(8,128)(2,1)S(1)} %get-tuple-element.115), channel_id=1, source_target_pairs={{0,1},{1,0},{2,3},{3,2},{4,5},{5,4},{6,7},{7,6},{8,9},{9,8},{10,11... | collective-permute-start | bytes 1572872 | tf_op jit(solution)/shard_map/ppermute | solution.py:35
  74.6 31.1 %collective-permute-start.3 = (bf16[512,512]{1,0:T(8,128)(2,1)S(1)}, bf16[512,512]{1,0:T(8,128)(2,1)S(1)}, u32[]{:S(2)}, u32[]{:S(2)}) collective-permute-start(bf16[512,512]{1,0:T(8,128)(2,1)S(1)} %get-tuple-element.115), channel_id=1, source_target_pairs={{0,2},{1,3},{2,0},{3,1},{4,6},{5,7},{6,4},{7,5},{8,10},{9,11},{10,... | collective-permute-start | bytes 1572872 | tf_op jit(solution)/shard_map/ppermute | solution.py:35
  84.8 0.8 copy-start.15
  85.6 9.1 %copy-start.16 = (bf16[512,512]{1,0:T(8,128)(2,1)}, bf16[512,512]{1,0:T(8,128)(2,1)S(1)}, u32[]{:S(2)}) copy-start(bf16[512,512]{1,0:T(8,128)(2,1)S(1)} %get-tuple-element.153) | copy-start | bytes 1572868
  94.7 23.0 %copy-start.5 = (bf16[512,512]{1,0:T(8,128)(2,1)}, bf16[512,512]{1,0:T(8,128)(2,1)S(1)}, u32[]{:S(2)}) copy-start(bf16[512,512]{1,0:T(8,128)(2,1)S(1)} %get-tuple-element.156) | copy-start | bytes 1572868
  94.7 23.0 %copy-start.7 = (bf16[512,512]{1,0:T(8,128)(2,1)}, bf16[512,512]{1,0:T(8,128)(2,1)S(1)}, u32[]{:S(2)}) copy-start(bf16[512,512]{1,0:T(8,128)(2,1)S(1)} %get-tuple-element.155) | copy-start | bytes 1572868
  105.6 23.6 %collective-permute-start.6 = (bf16[512,512]{1,0:T(8,128)(2,1)S(1)}, bf16[512,512]{1,0:T(8,128)(2,1)S(1)}, u32[]{:S(2)}, u32[]{:S(2)}) collective-permute-start(bf16[512,512]{1,0:T(8,128)(2,1)S(1)} %get-tuple-element.131), channel_id=1, source_target_pairs={{0,1},{1,0},{2,3},{3,2},{4,5},{5,4},{6,7},{7,6},{8,9},{9,8},{10,11... | collective-permute-start | bytes 1572872 | tf_op jit(solution)/shard_map/ppermute | solution.py:35
  107.1 24.8 %collective-permute-start.7 = (bf16[512,512]{1,0:T(8,128)(2,1)S(1)}, bf16[512,512]{1,0:T(8,128)(2,1)S(1)}, u32[]{:S(2)}, u32[]{:S(2)}) collective-permute-start(bf16[512,512]{1,0:T(8,128)(2,1)S(1)} %get-tuple-element.131), channel_id=1, source_target_pairs={{0,2},{1,3},{2,0},{3,1},{4,6},{5,7},{6,4},{7,5},{8,10},{9,11},{10,... | collective-permute-start | bytes 1572872 | tf_op jit(solution)/shard_map/ppermute | solution.py:35
  132.0 252.5 %reduce-scatter.5.cloned.1.call-start = ((), (), s32[]{:S(2)}) async-start(), calls=%async_computation.3 | async-start | bytes 14155776 | tf_op jit(solution)/shard_map/reduce_scatter | solution.py:167
  132.0 30.7 %collective-permute-start.14 = (bf16[512,512]{1,0:T(8,128)(2,1)}, bf16[512,512]{1,0:T(8,128)(2,1)S(1)}, u32[]{:S(2)}, u32[]{:S(2)}) collective-permute-start(bf16[512,512]{1,0:T(8,128)(2,1)} %get-tuple-element.152), channel_id=1, source_target_pairs={{0,1},{1,0},{2,3},{3,2},{4,5},{5,4},{6,7},{7,6},{8,9},{9,8},{10,11... | collective-permute-start | bytes 1572872 | tf_op jit(solution)/shard_map/ppermute | solution.py:35
  132.4 30.4 %collective-permute-start.15 = (bf16[512,512]{1,0:T(8,128)(2,1)}, bf16[512,512]{1,0:T(8,128)(2,1)S(1)}, u32[]{:S(2)}, u32[]{:S(2)}) collective-permute-start(bf16[512,512]{1,0:T(8,128)(2,1)} %get-tuple-element.152), channel_id=1, source_target_pairs={{0,2},{1,3},{2,0},{3,1},{4,6},{5,7},{6,4},{7,5},{8,10},{9,11},{10,... | collective-permute-start | bytes 1572872 | tf_op jit(solution)/shard_map/ppermute | solution.py:35
  135.1 46.4 %collective-permute-start.8 = (bf16[512,512]{1,0:T(8,128)(2,1)}, bf16[512,512]{1,0:T(8,128)(2,1)S(1)}, u32[]{:S(2)}, u32[]{:S(2)}) collective-permute-start(bf16[512,512]{1,0:T(8,128)(2,1)} %get-tuple-element.133), channel_id=1, source_target_pairs={{0,1},{1,0},{2,3},{3,2},{4,5},{5,4},{6,7},{7,6},{8,9},{9,8},{10,11... | collective-permute-start | bytes 1572872 | tf_op jit(solution)/shard_map/ppermute | solution.py:35
  135.2 47.1 %collective-permute-start.9 = (bf16[512,512]{1,0:T(8,128)(2,1)}, bf16[512,512]{1,0:T(8,128)(2,1)S(1)}, u32[]{:S(2)}, u32[]{:S(2)}) collective-permute-start(bf16[512,512]{1,0:T(8,128)(2,1)} %get-tuple-element.133), channel_id=1, source_target_pairs={{0,2},{1,3},{2,0},{3,1},{4,6},{5,7},{6,4},{7,5},{8,10},{9,11},{10,... | collective-permute-start | bytes 1572872 | tf_op jit(solution)/shard_map/ppermute | solution.py:35
  162.7 41.2 %collective-permute-start.16 = (bf16[512,512]{1,0:T(8,128)(2,1)}, bf16[512,512]{1,0:T(8,128)(2,1)S(1)}, u32[]{:S(2)}, u32[]{:S(2)}) collective-permute-start(bf16[512,512]{1,0:T(8,128)(2,1)} %copy-done.16), channel_id=1, source_target_pairs={{0,1},{1,0},{2,3},{3,2},{4,5},{5,4},{6,7},{7,6},{8,9},{9,8},{10,11... | collective-permute-start | bytes 1572872 | tf_op jit(solution)/shard_map/ppermute | solution.py:35
  162.8 42.0 %collective-permute-start.17 = (bf16[512,512]{1,0:T(8,128)(2,1)}, bf16[512,512]{1,0:T(8,128)(2,1)S(1)}, u32[]{:S(2)}, u32[]{:S(2)}) collective-permute-start(bf16[512,512]{1,0:T(8,128)(2,1)} %copy-done.15), channel_id=1, source_target_pairs={{0,2},{1,3},{2,0},{3,1},{4,6},{5,7},{6,4},{7,5},{8,10},{9,11},{10,... | collective-permute-start | bytes 1572872 | tf_op jit(solution)/shard_map/ppermute | solution.py:35
  166.4 15.8 %copy-start.19 = (bf16[512,512]{1,0:T(8,128)(2,1)S(1)}, bf16[512,512]{1,0:T(8,128)(2,1)}, u32[]{:S(2)}) copy-start(bf16[512,512]{1,0:T(8,128)(2,1)} %get-tuple-element.135) | copy-start | bytes 1572868
  166.4 38.3 %copy-start.8 = (bf16[512,512]{1,0:T(8,128)(2,1)S(1)}, bf16[512,512]{1,0:T(8,128)(2,1)}, u32[]{:S(2)}) copy-start(bf16[512,512]{1,0:T(8,128)(2,1)} %copy-done.7) | copy-start | bytes 1572868
  166.4 38.3 %copy-start.6 = (bf16[512,512]{1,0:T(8,128)(2,1)S(1)}, bf16[512,512]{1,0:T(8,128)(2,1)}, u32[]{:S(2)}) copy-start(bf16[512,512]{1,0:T(8,128)(2,1)} %copy-done.5) | copy-start | bytes 1572868
  175.5 0.8 copy-start.14
  176.3 31.2 %copy-start.12 = (bf16[512,512]{1,0:T(8,128)(2,1)}, bf16[512,512]{1,0:T(8,128)(2,1)S(1)}, u32[]{:S(2)}) copy-start(bf16[512,512]{1,0:T(8,128)(2,1)S(1)} %get-tuple-element.207) | copy-start | bytes 1572868
  182.2 44.1 %collective-permute-start.10 = (bf16[512,512]{1,0:T(8,128)(2,1)S(1)}, bf16[512,512]{1,0:T(8,128)(2,1)S(1)}, u32[]{:S(2)}, u32[]{:S(2)}) collective-permute-start(bf16[512,512]{1,0:T(8,128)(2,1)S(1)} %copy-done.19), channel_id=1, source_target_pairs={{0,1},{1,0},{2,3},{3,2},{4,5},{5,4},{6,7},{7,6},{8,9},{9,8},{10,11... | collective-permute-start | bytes 1572872 | tf_op jit(solution)/shard_map/ppermute | solution.py:35
  182.2 45.0 %collective-permute-start.11 = (bf16[512,512]{1,0:T(8,128)(2,1)S(1)}, bf16[512,512]{1,0:T(8,128)(2,1)S(1)}, u32[]{:S(2)}, u32[]{:S(2)}) collective-permute-start(bf16[512,512]{1,0:T(8,128)(2,1)S(1)} %copy-done.19), channel_id=1, source_target_pairs={{0,2},{1,3},{2,0},{3,1},{4,6},{5,7},{6,4},{7,5},{8,10},{9,11},{10,... | collective-permute-start | bytes 1572872 | tf_op jit(solution)/shard_map/ppermute | solution.py:35
  203.9 12.4 %copy-start.1 = (bf16[512,512]{1,0:T(8,128)(2,1)}, bf16[512,512]{1,0:T(8,128)(2,1)S(1)}, u32[]{:S(2)}) copy-start(bf16[512,512]{1,0:T(8,128)(2,1)S(1)} %collective-permute-done.16.refs_1_) | copy-start | bytes 1572868
  204.7 11.6 %copy-start.3 = (bf16[512,512]{1,0:T(8,128)(2,1)}, bf16[512,512]{1,0:T(8,128)(2,1)S(1)}, u32[]{:S(2)}) copy-start(bf16[512,512]{1,0:T(8,128)(2,1)S(1)} %collective-permute-done.17.refs_2_) | copy-start | bytes 1572868
  204.7 38.1 %collective-permute-start.18 = (bf16[512,512]{1,0:T(8,128)(2,1)S(1)}, bf16[512,512]{1,0:T(8,128)(2,1)S(1)}, u32[]{:S(2)}, u32[]{:S(2)}) collective-permute-start(bf16[512,512]{1,0:T(8,128)(2,1)S(1)} %copy-done.8), channel_id=1, source_target_pairs={{0,1},{1,0},{2,3},{3,2},{4,5},{5,4},{6,7},{7,6},{8,9},{9,8},{10,11... | collective-permute-start | bytes 1572872 | tf_op jit(solution)/shard_map/ppermute | solution.py:35
  204.7 41.6 %collective-permute-start.19 = (bf16[512,512]{1,0:T(8,128)(2,1)S(1)}, bf16[512,512]{1,0:T(8,128)(2,1)S(1)}, u32[]{:S(2)}, u32[]{:S(2)}) collective-permute-start(bf16[512,512]{1,0:T(8,128)(2,1)S(1)} %copy-done.6), channel_id=1, source_target_pairs={{0,2},{1,3},{2,0},{3,1},{4,6},{5,7},{6,4},{7,5},{8,10},{9,11},{10,... | collective-permute-start | bytes 1572872 | tf_op jit(solution)/shard_map/ppermute | solution.py:35
  216.3 9.3 %copy-start.17 = (bf16[512,512]{1,0:T(8,128)(2,1)}, bf16[512,512]{1,0:T(8,128)(2,1)S(1)}, u32[]{:S(2)}) copy-start(bf16[512,512]{1,0:T(8,128)(2,1)S(1)} %get-tuple-element.191) | copy-start | bytes 1572868
  216.3 9.3 %copy-start.18 = (bf16[512,512]{1,0:T(8,128)(2,1)}, bf16[512,512]{1,0:T(8,128)(2,1)S(1)}, u32[]{:S(2)}) copy-start(bf16[512,512]{1,0:T(8,128)(2,1)S(1)} %get-tuple-element.190) | copy-start | bytes 1572868
  225.6 29.9 %copy-start.9 = (bf16[512,512]{1,0:T(8,128)(2,1)}, bf16[512,512]{1,0:T(8,128)(2,1)S(1)}, u32[]{:S(2)}) copy-start(bf16[512,512]{1,0:T(8,128)(2,1)S(1)} %get-tuple-element.209) | copy-start | bytes 1572868
  225.6 29.9 %copy-start.10 = (bf16[512,512]{1,0:T(8,128)(2,1)}, bf16[512,512]{1,0:T(8,128)(2,1)S(1)}, u32[]{:S(2)}) copy-start(bf16[512,512]{1,0:T(8,128)(2,1)S(1)} %get-tuple-element.208) | copy-start | bytes 1572868
  255.5 0.8 copy-start.11
  256.3 0.8 copy-start.13
  257.1 29.5 %collective-permute-start.26 = (bf16[512,512]{1,0:T(8,128)(2,1)S(1)}, bf16[512,512]{1,0:T(8,128)(2,1)S(1)}, u32[]{:S(2)}, u32[]{:S(2)}) collective-permute-start(bf16[512,512]{1,0:T(8,128)(2,1)S(1)} %get-tuple-element.204), channel_id=1, source_target_pairs={{0,1},{1,0},{2,3},{3,2},{4,5},{5,4},{6,7},{7,6},{8,9},{9,8},{10,11... | collective-permute-start | bytes 1572872 | tf_op jit(solution)/shard_map/ppermute | solution.py:35
  257.2 29.4 %collective-permute-start.27 = (bf16[512,512]{1,0:T(8,128)(2,1)S(1)}, bf16[512,512]{1,0:T(8,128)(2,1)S(1)}, u32[]{:S(2)}, u32[]{:S(2)}) collective-permute-start(bf16[512,512]{1,0:T(8,128)(2,1)S(1)} %get-tuple-element.205), channel_id=1, source_target_pairs={{0,2},{1,3},{2,0},{3,1},{4,6},{5,7},{6,4},{7,5},{8,10},{9,11},{10,... | collective-permute-start | bytes 1572872 | tf_op jit(solution)/shard_map/ppermute | solution.py:35
  259.2 46.5 %collective-permute-start.20 = (bf16[512,512]{1,0:T(8,128)(2,1)S(1)}, bf16[512,512]{1,0:T(8,128)(2,1)S(1)}, u32[]{:S(2)}, u32[]{:S(2)}) collective-permute-start(bf16[512,512]{1,0:T(8,128)(2,1)S(1)} %get-tuple-element.188), channel_id=1, source_target_pairs={{0,1},{1,0},{2,3},{3,2},{4,5},{5,4},{6,7},{7,6},{8,9},{9,8},{10,11... | collective-permute-start | bytes 1572872 | tf_op jit(solution)/shard_map/ppermute | solution.py:35
  259.5 47.3 %collective-permute-start.21 = (bf16[512,512]{1,0:T(8,128)(2,1)S(1)}, bf16[512,512]{1,0:T(8,128)(2,1)S(1)}, u32[]{:S(2)}, u32[]{:S(2)}) collective-permute-start(bf16[512,512]{1,0:T(8,128)(2,1)S(1)} %get-tuple-element.189), channel_id=1, source_target_pairs={{0,2},{1,3},{2,0},{3,1},{4,6},{5,7},{6,4},{7,5},{8,10},{9,11},{10,... | collective-permute-start | bytes 1572872 | tf_op jit(solution)/shard_map/ppermute | solution.py:35
  286.6 41.5 %collective-permute-start.28 = (bf16[512,512]{1,0:T(8,128)(2,1)}, bf16[512,512]{1,0:T(8,128)(2,1)S(1)}, u32[]{:S(2)}, u32[]{:S(2)}) collective-permute-start(bf16[512,512]{1,0:T(8,128)(2,1)} %copy-done.14), channel_id=1, source_target_pairs={{0,1},{1,0},{2,3},{3,2},{4,5},{5,4},{6,7},{7,6},{8,9},{9,8},{10,11... | collective-permute-start | bytes 1572872 | tf_op jit(solution)/shard_map/ppermute | solution.py:35
  286.6 42.7 %collective-permute-start.29 = (bf16[512,512]{1,0:T(8,128)(2,1)}, bf16[512,512]{1,0:T(8,128)(2,1)S(1)}, u32[]{:S(2)}, u32[]{:S(2)}) collective-permute-start(bf16[512,512]{1,0:T(8,128)(2,1)} %copy-done.12), channel_id=1, source_target_pairs={{0,2},{1,3},{2,0},{3,1},{4,6},{5,7},{6,4},{7,5},{8,10},{9,11},{10,... | collective-permute-start | bytes 1572872 | tf_op jit(solution)/shard_map/ppermute | solution.py:35
  306.9 43.7 %collective-permute-start.22 = (bf16[512,512]{1,0:T(8,128)(2,1)}, bf16[512,512]{1,0:T(8,128)(2,1)S(1)}, u32[]{:S(2)}, u32[]{:S(2)}) collective-permute-start(bf16[512,512]{1,0:T(8,128)(2,1)} %copy-done.18), channel_id=1, source_target_pairs={{0,1},{1,0},{2,3},{3,2},{4,5},{5,4},{6,7},{7,6},{8,9},{9,8},{10,11... | collective-permute-start | bytes 1572872 | tf_op jit(solution)/shard_map/ppermute | solution.py:35
  306.9 45.0 %collective-permute-start.23 = (bf16[512,512]{1,0:T(8,128)(2,1)}, bf16[512,512]{1,0:T(8,128)(2,1)S(1)}, u32[]{:S(2)}, u32[]{:S(2)}) collective-permute-start(bf16[512,512]{1,0:T(8,128)(2,1)} %copy-done.17), channel_id=1, source_target_pairs={{0,2},{1,3},{2,0},{3,1},{4,6},{5,7},{6,4},{7,5},{8,10},{9,11},{10,... | collective-permute-start | bytes 1572872 | tf_op jit(solution)/shard_map/ppermute | solution.py:35
  329.4 60.1 %collective-permute-start.30 = (bf16[512,512]{1,0:T(8,128)(2,1)}, bf16[512,512]{1,0:T(8,128)(2,1)S(1)}, u32[]{:S(2)}, u32[]{:S(2)}) collective-permute-start(bf16[512,512]{1,0:T(8,128)(2,1)} %copy-done.10), channel_id=1, source_target_pairs={{0,1},{1,0},{2,3},{3,2},{4,5},{5,4},{6,7},{7,6},{8,9},{9,8},{10,11... | collective-permute-start | bytes 1572872 | tf_op jit(solution)/shard_map/ppermute | solution.py:35
  329.4 60.1 %collective-permute-start.31 = (bf16[512,512]{1,0:T(8,128)(2,1)}, bf16[512,512]{1,0:T(8,128)(2,1)S(1)}, u32[]{:S(2)}, u32[]{:S(2)}) collective-permute-start(bf16[512,512]{1,0:T(8,128)(2,1)} %copy-done.9), channel_id=1, source_target_pairs={{0,2},{1,3},{2,0},{3,1},{4,6},{5,7},{6,4},{7,5},{8,10},{9,11},{10,... | collective-permute-start | bytes 1572872 | tf_op jit(solution)/shard_map/ppermute | solution.py:35
  351.9 39.7 %collective-permute-start.24 = (bf16[512,512]{1,0:T(8,128)(2,1)}, bf16[512,512]{1,0:T(8,128)(2,1)S(1)}, u32[]{:S(2)}, u32[]{:S(2)}) collective-permute-start(bf16[512,512]{1,0:T(8,128)(2,1)} %copy-done.13), channel_id=1, source_target_pairs={{0,1},{1,0},{2,3},{3,2},{4,5},{5,4},{6,7},{7,6},{8,9},{9,8},{10,11... | collective-permute-start | bytes 1572872 | tf_op jit(solution)/shard_map/ppermute | solution.py:35
  351.9 40.1 %collective-permute-start.25 = (bf16[512,512]{1,0:T(8,128)(2,1)}, bf16[512,512]{1,0:T(8,128)(2,1)S(1)}, u32[]{:S(2)}, u32[]{:S(2)}) collective-permute-start(bf16[512,512]{1,0:T(8,128)(2,1)} %copy-done.11), channel_id=1, source_target_pairs={{0,2},{1,3},{2,0},{3,1},{4,6},{5,7},{6,4},{7,5},{8,10},{9,11},{10,... | collective-permute-start | bytes 1572872 | tf_op jit(solution)/shard_map/ppermute | solution.py:35
  354.0 2.2 copy-start
  356.2 15.2 %copy-start.2 = (bf16[512,512]{1,0:T(8,128)(2,1)S(1)}, bf16[512,512]{1,0:T(8,128)(2,1)}, u32[]{:S(2)}) copy-start(bf16[512,512]{1,0:T(8,128)(2,1)} %copy-done.1) | copy-start | bytes 1572868
  356.2 15.2 %copy-start.4 = (bf16[512,512]{1,0:T(8,128)(2,1)S(1)}, bf16[512,512]{1,0:T(8,128)(2,1)}, u32[]{:S(2)}) copy-start(bf16[512,512]{1,0:T(8,128)(2,1)} %copy-done.3) | copy-start | bytes 1572868
Sparse Core Ops, SparseCore 0:
  132.1 92.4 reduce-scatter.2
  257.2 91.4 reduce-scatter.4

commit v3 on v2

--- a/solution.py
+++ b/solution.py
@@ -133,7 +133,7 @@
             input_output_aliases=aliases,
             compiler_params=params,
             cost_estimate=pl.CostEstimate(
-                flops=2 * rows * width * width * (2 * partners + far),
+                flops=int(9 * 1.15e9),
                 bytes_accessed=moved,
                 transcendentals=rows * width,
             ),
@@ -181,7 +181,7 @@
         out_shape=jax.ShapeDtypeStruct(tokens.shape, jnp.float32),
         compiler_params=params,
         cost_estimate=pl.CostEstimate(
-            flops=2 * rows * width * width * near * blocks,
+            flops=int(200 * 1.15e9),
             bytes_accessed=blocks * near * 2 * width * (rows + width) + 4 * rows * width * blocks,
             transcendentals=0,
         ),
@@ -209,7 +209,7 @@
             input_output_aliases=aliases,
             compiler_params=params,
             cost_estimate=pl.CostEstimate(
-                flops=rows * width * far, bytes_accessed=rows * width * (6 + 2 * far), transcendentals=0
+                flops=int(25 * 1.15e9), bytes_accessed=rows * width * (6 + 2 * far), transcendentals=0
             ),
             name="last_step",
         )(*operands)

time: 402 us -> 391 us (0.973)
  waiting for transfers between devices: 229 us -> 215 us
    ppermute x32, waiting for transfers between devices: 229 us -> 210 us  [swapped(): return lax.ppermute(value, 'feat', pairs)]
    reduce_scatter x2, waiting for transfers between devices: 0.01 us -> 5.18 us  [local(): lax.psum_scatter(grads, 'dp', scatter_dimension=0, tiled=False)]
  transfers between devices with their start and end apart: 34 -> 34, of which waited for: 24 -> 25; matrix products, arithmetic and copies ran while one was open for 1% -> 1% of each run, Pallas kernels for 26% -> 27%
where the time goes in v3:
time: 391 us; the launch traced here: 390 us
  waiting for transfers between devices  215 us (55%)
  Pallas kernels  108 us (28%)
  starting transfers between devices  41.5 us (11%)
  between operations  14.2 us (4%)
  local copies, waits for them, and re-layouts  5.78 us (1%)
  other arithmetic  4.99 us (1%)
    ppermute x32, waiting for transfers between devices, swapped(): return lax.ppermute(value, 'feat', pairs)  210 us
    pallas_call x8, Pallas kernels, step(): pl.pallas_call(partial(block_step, partners, near, split), grid=(1,), in_...  73.1 us
    ppermute x32, starting transfers between devices, swapped(): return lax.ppermute(value, 'feat', pairs)  41.5 us
    pallas_call x8, Pallas kernels, local(): pl.pallas_call(partial(last_step, far), grid=(1,), in_specs=specs, out_sp...  18.3 us
    pallas_call x1, Pallas kernels, local(): pl.pallas_call(partial(near_step, near), grid=(blocks,), in_specs=[pl.Blo...  17 us
  transfers between devices with their start and end apart: 34, of which 25 were waited for; matrix products, arithmetic and copies ran while one was open for 1% of the time, Pallas kernels for 27%

profile of v3, /device:TPU:0, one launch (start us, length us, event | category | flops | bytes accessed | tf_op | source)
XLA Modules:
  0.0 390.3 jit_solution(3142425733537540397)
XLA Ops:
  7.2 3.5 fusion
  10.8 4.0 %collective-permute-start.5 = (bf16[512,512]{1,0:T(8,128)(2,1)S(1)}, bf16[512,512]{1,0:T(8,128)(2,1)S(1)}, u32[]{:S(2)}, u32[]{:S(2)}) collective-permute-start(bf16[512,512]{1,0:T(8,128)(2,1)S(1)} %get-tuple-element.228), channel_id=1, source_target_pairs={{0,2},{1,3},{2,0},{3,1},{4,6},{5,7},{6,4},{7,5},{8,10},{9,11},{10,... | collective-permute-start | bytes 1572872 | tf_op jit(solution)/shard_map/ppermute | solution.py:35
  14.8 1.6 collective-permute-start.4
  16.8 22.9 %collective-permute-done.5.refs_5_ = bf16[512,512]{1,0:T(8,128)(2,1)S(1)} collective-permute-done((bf16[512,512]{1,0:T(8,128)(2,1)S(1)}, bf16[512,512]{1,0:T(8,128)(2,1)S(1)}, u32[]{:S(2)}, u32[]{:S(2)}) %collective-permute-start.5) | collective-permute-done | bytes 524320 | tf_op jit(solution)/shard_map/ppermute | solution.py:35
  39.7 1.2 collective-permute-done.4.refs_4_
  40.9 2.5 collective-permute-start.13
  43.4 18.0 %collective-permute-done.1.refs_5_ = bf16[512,512]{1,0:T(8,128)(2,1)S(1)} collective-permute-done((bf16[512,512]{1,0:T(8,128)(2,1)S(1)}, bf16[512,512]{1,0:T(8,128)(2,1)S(1)}, u32[]{:S(2)}, u32[]{:S(2)}) %collective-permute-start.1) | collective-permute-done | bytes 524320 | tf_op jit(solution)/shard_map/ppermute | solution.py:35
  61.4 13.2 %collective-permute-done.refs_4_ = bf16[512,512]{1,0:T(8,128)(2,1)S(1)} collective-permute-done((bf16[512,512]{1,0:T(8,128)(2,1)S(1)}, bf16[512,512]{1,0:T(8,128)(2,1)S(1)}, u32[]{:S(2)}, u32[]{:S(2)}) %collective-permute-start) | collective-permute-done | bytes 524320 | tf_op jit(solution)/shard_map/ppermute | solution.py:35
  74.6 1.3 collective-permute-start.3
  75.9 9.0 %block_step.8 = (bf16[512,4096]{1,0:T(8,128)(2,1)}, bf16[512,4096]{1,0:T(8,128)(2,1)}, bf16[8,4,6,64,512]{4,3,2,1,0:T(8,128)(2,1)}, bf16[512,512]{1,0:T(8,128)(2,1)}, bf16[512,512]{1,0:T(8,128)(2,1)S(1)}) custom-call(bf16[512,4096]{1,0:T(8,128)(2,1)} %refs_3_.15, bf16[512,4096]{1,0:T(8,128)(2,1)} %refs_3_.15, bf16[512,4096]{1,0:T(8,128)(2,1)} %refs_3_.15, ...), custom_call_target="tpu_custom_call" | custom-call | flops 10350000128 | bytes 15204352 | tf_op jit(solution)/shard_map/block_step/pallas_call | solution.py:117
  84.9 8.9 %block_step.9 = (bf16[512,4096]{1,0:T(8,128)(2,1)}, bf16[512,4096]{1,0:T(8,128)(2,1)}, bf16[8,4,6,64,512]{4,3,2,1,0:T(8,128)(2,1)}, bf16[512,512]{1,0:T(8,128)(2,1)S(1)}, bf16[512,512]{1,0:T(8,128)(2,1)S(1)}) custom-call(bf16[512,4096]{1,0:T(8,128)(2,1)} %refs_3_.15, ...), custom_call_target="tpu_custom_call", output_to_operand_aliasing={{0}: (8, {}), {1}: (9, {}), {2}: (10, {})} | custom-call | flops 10350000128 | bytes 15204352 | tf_op jit(solution)/shard_map/block_step/pallas_call | solution.py:117
  93.8 2.1 collective-permute-done.12.refs_4_
  95.9 9.8 %collective-permute-done.2.refs_4_ = bf16[512,512]{1,0:T(8,128)(2,1)S(1)} collective-permute-done((bf16[512,512]{1,0:T(8,128)(2,1)S(1)}, bf16[512,512]{1,0:T(8,128)(2,1)S(1)}, u32[]{:S(2)}, u32[]{:S(2)}) %collective-permute-start.2) | collective-permute-done | bytes 524320 | tf_op jit(solution)/shard_map/ppermute | solution.py:35
  105.7 1.5 collective-permute-start.6
  107.1 1.6 collective-permute-start.7
  108.7 9.3 %block_step.10 = (bf16[512,4096]{1,0:T(8,128)(2,1)}, bf16[512,4096]{1,0:T(8,128)(2,1)}, bf16[8,4,6,64,512]{4,3,2,1,0:T(8,128)(2,1)}, bf16[512,512]{1,0:T(8,128)(2,1)}, bf16[512,512]{1,0:T(8,128)(2,1)}) custom-call(bf16[512,4096]{1,0:T(8,128)(2,1)} %refs_3_.15, ...), custom_call_target="tpu_custom_call", output_to_operand_aliasing={{0}: (8, {}), {1}: (9, {}), {2}: (10, {})} | custom-call | flops 10350000128 | bytes 15204352 | tf_op jit(solution)/shard_map/block_step/pallas_call | solution.py:117
  118.0 9.4 %block_step.11 = (bf16[512,4096]{1,0:T(8,128)(2,1)}, bf16[512,4096]{1,0:T(8,128)(2,1)}, bf16[8,4,6,64,512]{4,3,2,1,0:T(8,128)(2,1)}, bf16[512,512]{1,0:T(8,128)(2,1)}, bf16[512,512]{1,0:T(8,128)(2,1)}) custom-call(bf16[512,4096]{1,0:T(8,128)(2,1)} %refs_3_.15, ...), custom_call_target="tpu_custom_call", output_to_operand_aliasing={{0}: (8, {}), {1}: (9, {}), {2}: (10, {})} | custom-call | flops 10350000128 | bytes 15204352 | tf_op jit(solution)/shard_map/block_step/pallas_call | solution.py:117
  127.4 1.9 collective-permute-done.6.refs_4_
  129.3 2.7 collective-permute-done.7.refs_5_
  132.1 0.4 collective-permute-start.14
  132.4 2.7 collective-permute-start.15
  135.2 1.9 collective-permute-start.9
  137.1 25.5 %collective-permute-done.14.refs_4_ = bf16[512,512]{1,0:T(8,128)(2,1)S(1)} collective-permute-done((bf16[512,512]{1,0:T(8,128)(2,1)S(1)}, bf16[512,512]{1,0:T(8,128)(2,1)S(1)}, u32[]{:S(2)}, u32[]{:S(2)}) %collective-permute-start.14) | collective-permute-done | bytes 524320 | tf_op jit(solution)/shard_map/ppermute | solution.py:35
  162.5 3.6 collective-permute-start.17
  166.2 8.9 %block_step.12 = (bf16[512,4096]{1,0:T(8,128)(2,1)}, bf16[512,4096]{1,0:T(8,128)(2,1)}, bf16[8,4,6,64,512]{4,3,2,1,0:T(8,128)(2,1)}, bf16[512,512]{1,0:T(8,128)(2,1)S(1)}, bf16[512,512]{1,0:T(8,128)(2,1)S(1)}) custom-call(bf16[512,4096]{1,0:T(8,128)(2,1)} %refs_3_.15, bf16[512,4096]{1,0:T(8,128)(2,1)} %refs_3_.15, ...), custom_call_target="tpu_custom_call", output_to_operand_aliasing={{0}: (8, {}), {1}: (9, {})} | custom-call | flops 10350000128 | bytes 15204352 | tf_op jit(solution)/shard_map/block_step/pallas_call | solution.py:117
  175.1 9.3 %block_step.13 = (bf16[512,4096]{1,0:T(8,128)(2,1)}, bf16[512,4096]{1,0:T(8,128)(2,1)}, bf16[8,4,6,64,512]{4,3,2,1,0:T(8,128)(2,1)}, bf16[512,512]{1,0:T(8,128)(2,1)S(1)}, bf16[512,512]{1,0:T(8,128)(2,1)S(1)}) custom-call(bf16[512,4096]{1,0:T(8,128)(2,1)} %refs_3_.15, ...), custom_call_target="tpu_custom_call", output_to_operand_aliasing={{0}: (8, {}), {1}: (9, {}), {2}: (10, {})} | custom-call | flops 10350000128 | bytes 15204352 | tf_op jit(solution)/shard_map/block_step/pallas_call | solution.py:117
  184.5 1.4 collective-permute-start.11
  185.9 17.8 %collective-permute-done.16.refs_1_ = bf16[512,512]{1,0:T(8,128)(2,1)S(1)} collective-permute-done((bf16[512,512]{1,0:T(8,128)(2,1)}, bf16[512,512]{1,0:T(8,128)(2,1)S(1)}, u32[]{:S(2)}, u32[]{:S(2)}) %collective-permute-start.16) | collective-permute-done | bytes 524320 | tf_op jit(solution)/shard_map/ppermute | solution.py:35
  203.7 0.8 collective-permute-done.17.refs_2_
  204.5 2.8 collective-permute-start.19
  207.3 8.9 %block_step.14 = (bf16[512,4096]{1,0:T(8,128)(2,1)}, bf16[512,4096]{1,0:T(8,128)(2,1)}, bf16[8,4,6,64,512]{4,3,2,1,0:T(8,128)(2,1)}, bf16[512,512]{1,0:T(8,128)(2,1)S(1)}, bf16[512,512]{1,0:T(8,128)(2,1)S(1)}) custom-call(bf16[512,4096]{1,0:T(8,128)(2,1)} %refs_3_.15, ...), custom_call_target="tpu_custom_call", output_to_operand_aliasing={{0}: (8, {}), {1}: (9, {}), {2}: (10, {})} | custom-call | flops 10350000128 | bytes 15204352 | tf_op jit(solution)/shard_map/block_step/pallas_call | solution.py:117
  216.2 10.0 %collective-permute-done.10.refs_4_ = bf16[512,512]{1,0:T(8,128)(2,1)S(1)} collective-permute-done((bf16[512,512]{1,0:T(8,128)(2,1)S(1)}, bf16[512,512]{1,0:T(8,128)(2,1)S(1)}, u32[]{:S(2)}, u32[]{:S(2)}) %collective-permute-start.10) | collective-permute-done | bytes 524320 | tf_op jit(solution)/shard_map/ppermute | solution.py:35
  226.2 0.9 collective-permute-done.11.refs_5_
  227.1 2.8 collective-permute-start.27
  229.8 18.8 %collective-permute-done.18.refs_1_ = bf16[512,512]{1,0:T(8,128)(2,1)S(1)} collective-permute-done((bf16[512,512]{1,0:T(8,128)(2,1)S(1)}, bf16[512,512]{1,0:T(8,128)(2,1)S(1)}, u32[]{:S(2)}, u32[]{:S(2)}) %collective-permute-start.18) | collective-permute-done | bytes 524320 | tf_op jit(solution)/shard_map/ppermute | solution.py:35
  248.6 1.0 collective-permute-done.19.refs_2_
  249.6 2.8 collective-permute-start.21
  252.3 9.5 %block_step.15 = (bf16[512,4096]{1,0:T(8,128)(2,1)}, bf16[512,4096]{1,0:T(8,128)(2,1)}, bf16[8,4,6,64,512]{4,3,2,1,0:T(8,128)(2,1)}, bf16[512,512]{1,0:T(8,128)(2,1)}, bf16[512,512]{1,0:T(8,128)(2,1)}) custom-call(bf16[512,4096]{1,0:T(8,128)(2,1)} %refs_3_.15, ...), custom_call_target="tpu_custom_call", output_to_operand_aliasing={{0}: (8, {}), {1}: (9, {}), {2}: (10, {})} | custom-call | flops 10350000128 | bytes 15204352 | tf_op jit(solution)/shard_map/block_step/pallas_call | solution.py:117
  261.9 2.2 copy-done
  264.0 17.0 %near_step.1.refs_0_ = f32[512,4096]{1,0:T(8,128)} custom-call(bf16[512,4096]{1,0:T(8,128)(2,1)S(1)} %copy-done, bf16[512,4096]{1,0:T(8,128)(2,1)S(1)} %copy-done, bf16[512,4096]{1,0:T(8,128)(2,1)S(1)} %copy-done, bf16[512,4096]{1,0:T(8,128)(2,1)S(1)} %copy-done, bf16[8,6,512,512]{3,2,1,0:T(8,128)(2,1)} %refs_7_.17, bf16[8,6,512,512]{3,2,1,0:T(8,128)(2,1)} %refs_7_.17, ...), custom_call_target="tpu_custom_call" | custom-call | flops 230000001024 | bytes 41943040 | tf_op jit(solution)/shard_map/near_step/pallas_call | solution.py:169
  281.1 2.3 last_step.8.refs_3_
  283.4 2.2 last_step.9.refs_3_
  285.7 2.0 collective-permute-done.20.refs_1_
  287.7 3.9 collective-permute-done.21.refs_2_
  291.6 1.2 collective-permute-start.29
  292.8 1.7 collective-permute-start.22
  294.5 2.0 collective-permute-start.23
  296.6 2.5 last_step.10.refs_3_
  299.0 2.5 last_step.11.refs_3_
  301.6 18.3 %collective-permute-done.28.refs_1_ = bf16[512,512]{1,0:T(8,128)(2,1)S(1)} collective-permute-done((bf16[512,512]{1,0:T(8,128)(2,1)S(1)}, bf16[512,512]{1,0:T(8,128)(2,1)S(1)}, u32[]{:S(2)}, u32[]{:S(2)}) %collective-permute-start.28) | collective-permute-done | bytes 524320 | tf_op jit(solution)/shard_map/ppermute | solution.py:35
  319.9 2.3 collective-permute-start.31
  322.2 18.5 %collective-permute-done.22.refs_1_ = bf16[512,512]{1,0:T(8,128)(2,1)S(1)} collective-permute-done((bf16[512,512]{1,0:T(8,128)(2,1)S(1)}, bf16[512,512]{1,0:T(8,128)(2,1)S(1)}, u32[]{:S(2)}, u32[]{:S(2)}) %collective-permute-start.22) | collective-permute-done | bytes 524320 | tf_op jit(solution)/shard_map/ppermute | solution.py:35
  340.7 0.6 collective-permute-done.23.refs_2_
  341.3 2.8 collective-permute-start.25
  344.1 2.2 last_step.12.refs_3_
  346.3 2.2 last_step.13.refs_3_
  348.5 5.2 %reduce-scatter.5.cloned.1.call-done = bf16[1,4,6,64,512]{4,3,2,1,0:T(8,128)(2,1)} async-done(((bf16[8,4,6,64,512]{4,3,2,1,0:T(8,128)(2,1)}), bf16[1,4,6,64,512]{4,3,2,1,0:T(8,128)(2,1)}) %reduce-scatter.5.cloned.1.call-update) | async-done | bytes 1572880 | tf_op jit(solution)/shard_map/reduce_scatter | solution.py:167
  353.7 5.0 %maximum_convert_fusion = f32[8,6,64,512]{3,2,1,0:T(8,128)} fusion(bf16[4,6,64,512]{3,2,1,0:T(8,128)(2,1)} %bitcast.3, bf16[4,6,64,512]{3,2,1,0:T(8,128)(2,1)} %bitcast.2), kind=kLoop, calls=%fused_computation | loop fusion | flops 3145728 | bytes 9437184 | tf_op jit(solution)/shard_map/convert_element_type | solution.py:191
  358.7 4.5 %collective-permute-done.30.refs_1_ = bf16[512,512]{1,0:T(8,128)(2,1)S(1)} collective-permute-done((bf16[512,512]{1,0:T(8,128)(2,1)S(1)}, bf16[512,512]{1,0:T(8,128)(2,1)S(1)}, u32[]{:S(2)}, u32[]{:S(2)}) %collective-permute-start.30) | collective-permute-done | bytes 524320 | tf_op jit(solution)/shard_map/ppermute | solution.py:35
  363.1 0.7 collective-permute-done.31.refs_2_
  363.8 2.2 last_step.14.refs_3_
  366.0 12.8 %collective-permute-done.24.refs_1_ = bf16[512,512]{1,0:T(8,128)(2,1)S(1)} collective-permute-done((bf16[512,512]{1,0:T(8,128)(2,1)}, bf16[512,512]{1,0:T(8,128)(2,1)S(1)}, u32[]{:S(2)}, u32[]{:S(2)}) %collective-permute-start.24) | collective-permute-done | bytes 524320 | tf_op jit(solution)/shard_map/ppermute | solution.py:35
  378.8 2.5 collective-permute-done.25.refs_2_
  381.3 2.2 last_step.15
  (53 shorter events, 0.9 us)
Async XLA Ops:
  7.2 341.3 %reduce-scatter.3.cloned.1.call-start = ((), (), s32[]{:S(2)}) async-start(), calls=%async_computation.2 | async-start | bytes 14155776 | tf_op jit(solution)/shard_map/reduce_scatter | solution.py:167
  10.8 28.9 %collective-permute-start.5 = (bf16[512,512]{1,0:T(8,128)(2,1)S(1)}, bf16[512,512]{1,0:T(8,128)(2,1)S(1)}, u32[]{:S(2)}, u32[]{:S(2)}) collective-permute-start(bf16[512,512]{1,0:T(8,128)(2,1)S(1)} %get-tuple-element.228), channel_id=1, source_target_pairs={{0,2},{1,3},{2,0},{3,1},{4,6},{5,7},{6,4},{7,5},{8,10},{9,11},{10,... | collective-permute-start | bytes 1572872 | tf_op jit(solution)/shard_map/ppermute | solution.py:35
  14.8 26.1 %collective-permute-start.4 = (bf16[512,512]{1,0:T(8,128)(2,1)S(1)}, bf16[512,512]{1,0:T(8,128)(2,1)S(1)}, u32[]{:S(2)}, u32[]{:S(2)}) collective-permute-start(bf16[512,512]{1,0:T(8,128)(2,1)S(1)} %get-tuple-element.228), channel_id=1, source_target_pairs={{0,1},{1,0},{2,3},{3,2},{4,5},{5,4},{6,7},{7,6},{8,9},{9,8},{10,11... | collective-permute-start | bytes 1572872 | tf_op jit(solution)/shard_map/ppermute | solution.py:35
  16.4 45.0 %collective-permute-start.1 = (bf16[512,512]{1,0:T(8,128)(2,1)S(1)}, bf16[512,512]{1,0:T(8,128)(2,1)S(1)}, u32[]{:S(2)}, u32[]{:S(2)}) collective-permute-start(bf16[512,512]{1,0:T(8,128)(2,1)S(1)} %get-tuple-element.230), channel_id=1, source_target_pairs={{0,2},{1,3},{2,0},{3,1},{4,6},{5,7},{6,4},{7,5},{8,10},{9,11},{10,... | collective-permute-start | bytes 1572872 | tf_op jit(solution)/shard_map/ppermute | solution.py:35
  16.7 57.9 %collective-permute-start = (bf16[512,512]{1,0:T(8,128)(2,1)S(1)}, bf16[512,512]{1,0:T(8,128)(2,1)S(1)}, u32[]{:S(2)}, u32[]{:S(2)}) collective-permute-start(bf16[512,512]{1,0:T(8,128)(2,1)S(1)} %get-tuple-element.230), channel_id=1, source_target_pairs={{0,1},{1,0},{2,3},{3,2},{4,5},{5,4},{6,7},{7,6},{8,9},{9,8},{10,11... | collective-permute-start | bytes 1572872 | tf_op jit(solution)/shard_map/ppermute | solution.py:35
  40.9 55.0 %collective-permute-start.12 = (bf16[512,512]{1,0:T(8,128)(2,1)S(1)}, bf16[512,512]{1,0:T(8,128)(2,1)S(1)}, u32[]{:S(2)}, u32[]{:S(2)}) collective-permute-start(bf16[512,512]{1,0:T(8,128)(2,1)S(1)} %get-tuple-element.139), channel_id=1, source_target_pairs={{0,1},{1,0},{2,3},{3,2},{4,5},{5,4},{6,7},{7,6},{8,9},{9,8},{10,11... | collective-permute-start | bytes 1572872 | tf_op jit(solution)/shard_map/ppermute | solution.py:35
  40.9 55.0 %collective-permute-start.13 = (bf16[512,512]{1,0:T(8,128)(2,1)S(1)}, bf16[512,512]{1,0:T(8,128)(2,1)S(1)}, u32[]{:S(2)}, u32[]{:S(2)}) collective-permute-start(bf16[512,512]{1,0:T(8,128)(2,1)S(1)} %get-tuple-element.139), channel_id=1, source_target_pairs={{0,2},{1,3},{2,0},{3,1},{4,6},{5,7},{6,4},{7,5},{8,10},{9,11},{10,... | collective-permute-start | bytes 1572872 | tf_op jit(solution)/shard_map/ppermute | solution.py:35
  74.6 31.1 %collective-permute-start.2 = (bf16[512,512]{1,0:T(8,128)(2,1)S(1)}, bf16[512,512]{1,0:T(8,128)(2,1)S(1)}, u32[]{:S(2)}, u32[]{:S(2)}) collective-permute-start(bf16[512,512]{1,0:T(8,128)(2,1)S(1)} %get-tuple-element.115), channel_id=1, source_target_pairs={{0,1},{1,0},{2,3},{3,2},{4,5},{5,4},{6,7},{7,6},{8,9},{9,8},{10,11... | collective-permute-start | bytes 1572872 | tf_op jit(solution)/shard_map/ppermute | solution.py:35
  74.6 31.1 %collective-permute-start.3 = (bf16[512,512]{1,0:T(8,128)(2,1)S(1)}, bf16[512,512]{1,0:T(8,128)(2,1)S(1)}, u32[]{:S(2)}, u32[]{:S(2)}) collective-permute-start(bf16[512,512]{1,0:T(8,128)(2,1)S(1)} %get-tuple-element.115), channel_id=1, source_target_pairs={{0,2},{1,3},{2,0},{3,1},{4,6},{5,7},{6,4},{7,5},{8,10},{9,11},{10,... | collective-permute-start | bytes 1572872 | tf_op jit(solution)/shard_map/ppermute | solution.py:35
  105.7 23.6 %collective-permute-start.6 = (bf16[512,512]{1,0:T(8,128)(2,1)S(1)}, bf16[512,512]{1,0:T(8,128)(2,1)S(1)}, u32[]{:S(2)}, u32[]{:S(2)}) collective-permute-start(bf16[512,512]{1,0:T(8,128)(2,1)S(1)} %get-tuple-element.131), channel_id=1, source_target_pairs={{0,1},{1,0},{2,3},{3,2},{4,5},{5,4},{6,7},{7,6},{8,9},{9,8},{10,11... | collective-permute-start | bytes 1572872 | tf_op jit(solution)/shard_map/ppermute | solution.py:35
  107.1 24.8 %collective-permute-start.7 = (bf16[512,512]{1,0:T(8,128)(2,1)S(1)}, bf16[512,512]{1,0:T(8,128)(2,1)S(1)}, u32[]{:S(2)}, u32[]{:S(2)}) collective-permute-start(bf16[512,512]{1,0:T(8,128)(2,1)S(1)} %get-tuple-element.131), channel_id=1, source_target_pairs={{0,2},{1,3},{2,0},{3,1},{4,6},{5,7},{6,4},{7,5},{8,10},{9,11},{10,... | collective-permute-start | bytes 1572872 | tf_op jit(solution)/shard_map/ppermute | solution.py:35
  132.0 221.7 %reduce-scatter.5.cloned.1.call-start = ((), (), s32[]{:S(2)}) async-start(), calls=%async_computation.3 | async-start | bytes 14155776 | tf_op jit(solution)/shard_map/reduce_scatter | solution.py:167
  132.1 30.5 %collective-permute-start.14 = (bf16[512,512]{1,0:T(8,128)(2,1)S(1)}, bf16[512,512]{1,0:T(8,128)(2,1)S(1)}, u32[]{:S(2)}, u32[]{:S(2)}) collective-permute-start(bf16[512,512]{1,0:T(8,128)(2,1)S(1)} %get-tuple-element.152), channel_id=1, source_target_pairs={{0,1},{1,0},{2,3},{3,2},{4,5},{5,4},{6,7},{7,6},{8,9},{9,8},{10,11... | collective-permute-start | bytes 1572872 | tf_op jit(solution)/shard_map/ppermute | solution.py:35
  132.4 30.1 %collective-permute-start.15 = (bf16[512,512]{1,0:T(8,128)(2,1)S(1)}, bf16[512,512]{1,0:T(8,128)(2,1)S(1)}, u32[]{:S(2)}, u32[]{:S(2)}) collective-permute-start(bf16[512,512]{1,0:T(8,128)(2,1)S(1)} %get-tuple-element.152), channel_id=1, source_target_pairs={{0,2},{1,3},{2,0},{3,1},{4,6},{5,7},{6,4},{7,5},{8,10},{9,11},{10,... | collective-permute-start | bytes 1572872 | tf_op jit(solution)/shard_map/ppermute | solution.py:35
  135.1 49.3 %collective-permute-start.8 = (bf16[512,512]{1,0:T(8,128)(2,1)}, bf16[512,512]{1,0:T(8,128)(2,1)S(1)}, u32[]{:S(2)}, u32[]{:S(2)}) collective-permute-start(bf16[512,512]{1,0:T(8,128)(2,1)} %get-tuple-element.133), channel_id=1, source_target_pairs={{0,1},{1,0},{2,3},{3,2},{4,5},{5,4},{6,7},{7,6},{8,9},{9,8},{10,11... | collective-permute-start | bytes 1572872 | tf_op jit(solution)/shard_map/ppermute | solution.py:35
  135.2 49.2 %collective-permute-start.9 = (bf16[512,512]{1,0:T(8,128)(2,1)}, bf16[512,512]{1,0:T(8,128)(2,1)S(1)}, u32[]{:S(2)}, u32[]{:S(2)}) collective-permute-start(bf16[512,512]{1,0:T(8,128)(2,1)} %get-tuple-element.133), channel_id=1, source_target_pairs={{0,2},{1,3},{2,0},{3,1},{4,6},{5,7},{6,4},{7,5},{8,10},{9,11},{10,... | collective-permute-start | bytes 1572872 | tf_op jit(solution)/shard_map/ppermute | solution.py:35
  162.5 41.2 %collective-permute-start.16 = (bf16[512,512]{1,0:T(8,128)(2,1)}, bf16[512,512]{1,0:T(8,128)(2,1)S(1)}, u32[]{:S(2)}, u32[]{:S(2)}) collective-permute-start(bf16[512,512]{1,0:T(8,128)(2,1)} %get-tuple-element.153), channel_id=1, source_target_pairs={{0,1},{1,0},{2,3},{3,2},{4,5},{5,4},{6,7},{7,6},{8,9},{9,8},{10,11... | collective-permute-start | bytes 1572872 | tf_op jit(solution)/shard_map/ppermute | solution.py:35
  162.5 42.0 %collective-permute-start.17 = (bf16[512,512]{1,0:T(8,128)(2,1)S(1)}, bf16[512,512]{1,0:T(8,128)(2,1)S(1)}, u32[]{:S(2)}, u32[]{:S(2)}) collective-permute-start(bf16[512,512]{1,0:T(8,128)(2,1)S(1)} %get-tuple-element.154), channel_id=1, source_target_pairs={{0,2},{1,3},{2,0},{3,1},{4,6},{5,7},{6,4},{7,5},{8,10},{9,11},{10,... | collective-permute-start | bytes 1572872 | tf_op jit(solution)/shard_map/ppermute | solution.py:35
  175.1 9.3 %copy-start.1 = (bf16[512,512]{1,0:T(8,128)(2,1)}, bf16[512,512]{1,0:T(8,128)(2,1)S(1)}, u32[]{:S(2)}) copy-start(bf16[512,512]{1,0:T(8,128)(2,1)S(1)} %get-tuple-element.206) | copy-start | bytes 1572868
  175.1 9.3 %copy-start.13 = (bf16[512,512]{1,0:T(8,128)(2,1)S(1)}, bf16[512,512]{1,0:T(8,128)(2,1)}, u32[]{:S(2)}) copy-start(bf16[512,512]{1,0:T(8,128)(2,1)} %get-tuple-element.135) | copy-start | bytes 1572868
  184.4 41.7 %collective-permute-start.10 = (bf16[512,512]{1,0:T(8,128)(2,1)S(1)}, bf16[512,512]{1,0:T(8,128)(2,1)S(1)}, u32[]{:S(2)}, u32[]{:S(2)}) collective-permute-start(bf16[512,512]{1,0:T(8,128)(2,1)S(1)} %copy-done.13), channel_id=1, source_target_pairs={{0,1},{1,0},{2,3},{3,2},{4,5},{5,4},{6,7},{7,6},{8,9},{9,8},{10,11... | collective-permute-start | bytes 1572872 | tf_op jit(solution)/shard_map/ppermute | solution.py:35
  184.5 42.5 %collective-permute-start.11 = (bf16[512,512]{1,0:T(8,128)(2,1)S(1)}, bf16[512,512]{1,0:T(8,128)(2,1)S(1)}, u32[]{:S(2)}, u32[]{:S(2)}) collective-permute-start(bf16[512,512]{1,0:T(8,128)(2,1)S(1)} %copy-done.13), channel_id=1, source_target_pairs={{0,2},{1,3},{2,0},{3,1},{4,6},{5,7},{6,4},{7,5},{8,10},{9,11},{10,... | collective-permute-start | bytes 1572872 | tf_op jit(solution)/shard_map/ppermute | solution.py:35
  203.7 12.4 %copy-start.5 = (bf16[512,512]{1,0:T(8,128)(2,1)}, bf16[512,512]{1,0:T(8,128)(2,1)S(1)}, u32[]{:S(2)}) copy-start(bf16[512,512]{1,0:T(8,128)(2,1)S(1)} %collective-permute-done.16.refs_1_) | copy-start | bytes 1572868
  204.5 11.6 %copy-start.7 = (bf16[512,512]{1,0:T(8,128)(2,1)}, bf16[512,512]{1,0:T(8,128)(2,1)S(1)}, u32[]{:S(2)}) copy-start(bf16[512,512]{1,0:T(8,128)(2,1)S(1)} %collective-permute-done.17.refs_2_) | copy-start | bytes 1572868
  204.5 44.1 %collective-permute-start.18 = (bf16[512,512]{1,0:T(8,128)(2,1)S(1)}, bf16[512,512]{1,0:T(8,128)(2,1)S(1)}, u32[]{:S(2)}, u32[]{:S(2)}) collective-permute-start(bf16[512,512]{1,0:T(8,128)(2,1)S(1)} %get-tuple-element.155), channel_id=1, source_target_pairs={{0,1},{1,0},{2,3},{3,2},{4,5},{5,4},{6,7},{7,6},{8,9},{9,8},{10,11... | collective-permute-start | bytes 1572872 | tf_op jit(solution)/shard_map/ppermute | solution.py:35
  204.5 45.0 %collective-permute-start.19 = (bf16[512,512]{1,0:T(8,128)(2,1)S(1)}, bf16[512,512]{1,0:T(8,128)(2,1)S(1)}, u32[]{:S(2)}, u32[]{:S(2)}) collective-permute-start(bf16[512,512]{1,0:T(8,128)(2,1)S(1)} %get-tuple-element.156), channel_id=1, source_target_pairs={{0,2},{1,3},{2,0},{3,1},{4,6},{5,7},{6,4},{7,5},{8,10},{9,11},{10,... | collective-permute-start | bytes 1572872 | tf_op jit(solution)/shard_map/ppermute | solution.py:35
  216.2 45.6 %copy-start.3 = (bf16[512,512]{1,0:T(8,128)(2,1)}, bf16[512,512]{1,0:T(8,128)(2,1)S(1)}, u32[]{:S(2)}) copy-start(bf16[512,512]{1,0:T(8,128)(2,1)S(1)} %get-tuple-element.208) | copy-start | bytes 1572868
  227.0 64.5 %collective-permute-start.26 = (bf16[512,512]{1,0:T(8,128)(2,1)}, bf16[512,512]{1,0:T(8,128)(2,1)}, u32[]{:S(2)}, u32[]{:S(2)}) collective-permute-start(bf16[512,512]{1,0:T(8,128)(2,1)} %get-tuple-element.204), channel_id=1, source_target_pairs={{0,1},{1,0},{2,3},{3,2},{4,5},{5,4},{6,7},{7,6},{8,9},{9,8},{10,11... | collective-permute-start | bytes 1572872 | tf_op jit(solution)/shard_map/ppermute | solution.py:35
  227.1 64.5 %collective-permute-start.27 = (bf16[512,512]{1,0:T(8,128)(2,1)}, bf16[512,512]{1,0:T(8,128)(2,1)}, u32[]{:S(2)}, u32[]{:S(2)}) collective-permute-start(bf16[512,512]{1,0:T(8,128)(2,1)} %get-tuple-element.205), channel_id=1, source_target_pairs={{0,2},{1,3},{2,0},{3,1},{4,6},{5,7},{6,4},{7,5},{8,10},{9,11},{10,... | collective-permute-start | bytes 1572872 | tf_op jit(solution)/shard_map/ppermute | solution.py:35
  248.6 13.2 %copy-start.9 = (bf16[512,512]{1,0:T(8,128)(2,1)}, bf16[512,512]{1,0:T(8,128)(2,1)S(1)}, u32[]{:S(2)}) copy-start(bf16[512,512]{1,0:T(8,128)(2,1)S(1)} %collective-permute-done.18.refs_1_) | copy-start | bytes 1572868
  249.6 12.3 %copy-start.11 = (bf16[512,512]{1,0:T(8,128)(2,1)}, bf16[512,512]{1,0:T(8,128)(2,1)S(1)}, u32[]{:S(2)}) copy-start(bf16[512,512]{1,0:T(8,128)(2,1)S(1)} %collective-permute-done.19.refs_2_) | copy-start | bytes 1572868
  249.6 38.1 %collective-permute-start.20 = (bf16[512,512]{1,0:T(8,128)(2,1)}, bf16[512,512]{1,0:T(8,128)(2,1)}, u32[]{:S(2)}, u32[]{:S(2)}) collective-permute-start(bf16[512,512]{1,0:T(8,128)(2,1)} %get-tuple-element.188), channel_id=1, source_target_pairs={{0,1},{1,0},{2,3},{3,2},{4,5},{5,4},{6,7},{7,6},{8,9},{9,8},{10,11... | collective-permute-start | bytes 1572872 | tf_op jit(solution)/shard_map/ppermute | solution.py:35
  249.6 42.0 %collective-permute-start.21 = (bf16[512,512]{1,0:T(8,128)(2,1)}, bf16[512,512]{1,0:T(8,128)(2,1)}, u32[]{:S(2)}, u32[]{:S(2)}) collective-permute-start(bf16[512,512]{1,0:T(8,128)(2,1)} %get-tuple-element.189), channel_id=1, source_target_pairs={{0,2},{1,3},{2,0},{3,1},{4,6},{5,7},{6,4},{7,5},{8,10},{9,11},{10,... | collective-permute-start | bytes 1572872 | tf_op jit(solution)/shard_map/ppermute | solution.py:35
  261.8 2.2 copy-start
  264.0 17.0 %copy-start.6 = (bf16[512,512]{1,0:T(8,128)(2,1)S(1)}, bf16[512,512]{1,0:T(8,128)(2,1)}, u32[]{:S(2)}) copy-start(bf16[512,512]{1,0:T(8,128)(2,1)} %copy-done.5) | copy-start | bytes 1572868
  264.0 17.0 %copy-start.8 = (bf16[512,512]{1,0:T(8,128)(2,1)S(1)}, bf16[512,512]{1,0:T(8,128)(2,1)}, u32[]{:S(2)}) copy-start(bf16[512,512]{1,0:T(8,128)(2,1)} %copy-done.7) | copy-start | bytes 1572868
  281.1 2.4 copy-start.10
  281.1 2.4 copy-start.12
  283.4 8.1 %copy-start.2 = (bf16[512,512]{1,0:T(8,128)(2,1)S(1)}, bf16[512,512]{1,0:T(8,128)(2,1)}, u32[]{:S(2)}) copy-start(bf16[512,512]{1,0:T(8,128)(2,1)} %copy-done.1) | copy-start | bytes 1572868
  291.5 28.4 %collective-permute-start.28 = (bf16[512,512]{1,0:T(8,128)(2,1)S(1)}, bf16[512,512]{1,0:T(8,128)(2,1)S(1)}, u32[]{:S(2)}, u32[]{:S(2)}) collective-permute-start(bf16[512,512]{1,0:T(8,128)(2,1)S(1)} %copy-done.2), channel_id=1, source_target_pairs={{0,1},{1,0},{2,3},{3,2},{4,5},{5,4},{6,7},{7,6},{8,9},{9,8},{10,11... | collective-permute-start | bytes 1572872 | tf_op jit(solution)/shard_map/ppermute | solution.py:35
  291.6 28.3 %collective-permute-start.29 = (bf16[512,512]{1,0:T(8,128)(2,1)S(1)}, bf16[512,512]{1,0:T(8,128)(2,1)S(1)}, u32[]{:S(2)}, u32[]{:S(2)}) collective-permute-start(bf16[512,512]{1,0:T(8,128)(2,1)S(1)} %get-tuple-element.207), channel_id=1, source_target_pairs={{0,2},{1,3},{2,0},{3,1},{4,6},{5,7},{6,4},{7,5},{8,10},{9,11},{10,... | collective-permute-start | bytes 1572872 | tf_op jit(solution)/shard_map/ppermute | solution.py:35
  292.8 47.8 %collective-permute-start.22 = (bf16[512,512]{1,0:T(8,128)(2,1)S(1)}, bf16[512,512]{1,0:T(8,128)(2,1)S(1)}, u32[]{:S(2)}, u32[]{:S(2)}) collective-permute-start(bf16[512,512]{1,0:T(8,128)(2,1)S(1)} %get-tuple-element.190), channel_id=1, source_target_pairs={{0,1},{1,0},{2,3},{3,2},{4,5},{5,4},{6,7},{7,6},{8,9},{9,8},{10,11... | collective-permute-start | bytes 1572872 | tf_op jit(solution)/shard_map/ppermute | solution.py:35
  294.5 46.8 %collective-permute-start.23 = (bf16[512,512]{1,0:T(8,128)(2,1)S(1)}, bf16[512,512]{1,0:T(8,128)(2,1)S(1)}, u32[]{:S(2)}, u32[]{:S(2)}) collective-permute-start(bf16[512,512]{1,0:T(8,128)(2,1)S(1)} %get-tuple-element.191), channel_id=1, source_target_pairs={{0,2},{1,3},{2,0},{3,1},{4,6},{5,7},{6,4},{7,5},{8,10},{9,11},{10,... | collective-permute-start | bytes 1572872 | tf_op jit(solution)/shard_map/ppermute | solution.py:35
  299.0 20.9 %copy-start.4 = (bf16[512,512]{1,0:T(8,128)(2,1)S(1)}, bf16[512,512]{1,0:T(8,128)(2,1)}, u32[]{:S(2)}) copy-start(bf16[512,512]{1,0:T(8,128)(2,1)} %copy-done.3) | copy-start | bytes 1572868
  319.9 43.2 %collective-permute-start.30 = (bf16[512,512]{1,0:T(8,128)(2,1)S(1)}, bf16[512,512]{1,0:T(8,128)(2,1)S(1)}, u32[]{:S(2)}, u32[]{:S(2)}) collective-permute-start(bf16[512,512]{1,0:T(8,128)(2,1)S(1)} %copy-done.4), channel_id=1, source_target_pairs={{0,1},{1,0},{2,3},{3,2},{4,5},{5,4},{6,7},{7,6},{8,9},{9,8},{10,11... | collective-permute-start | bytes 1572872 | tf_op jit(solution)/shard_map/ppermute | solution.py:35
  319.9 43.9 %collective-permute-start.31 = (bf16[512,512]{1,0:T(8,128)(2,1)S(1)}, bf16[512,512]{1,0:T(8,128)(2,1)S(1)}, u32[]{:S(2)}, u32[]{:S(2)}) collective-permute-start(bf16[512,512]{1,0:T(8,128)(2,1)S(1)} %get-tuple-element.209), channel_id=1, source_target_pairs={{0,2},{1,3},{2,0},{3,1},{4,6},{5,7},{6,4},{7,5},{8,10},{9,11},{10,... | collective-permute-start | bytes 1572872 | tf_op jit(solution)/shard_map/ppermute | solution.py:35
  341.3 37.5 %collective-permute-start.24 = (bf16[512,512]{1,0:T(8,128)(2,1)}, bf16[512,512]{1,0:T(8,128)(2,1)S(1)}, u32[]{:S(2)}, u32[]{:S(2)}) collective-permute-start(bf16[512,512]{1,0:T(8,128)(2,1)} %get-tuple-element.192), channel_id=1, source_target_pairs={{0,1},{1,0},{2,3},{3,2},{4,5},{5,4},{6,7},{7,6},{8,9},{9,8},{10,11... | collective-permute-start | bytes 1572872 | tf_op jit(solution)/shard_map/ppermute | solution.py:35
  341.3 40.0 %collective-permute-start.25 = (bf16[512,512]{1,0:T(8,128)(2,1)}, bf16[512,512]{1,0:T(8,128)(2,1)S(1)}, u32[]{:S(2)}, u32[]{:S(2)}) collective-permute-start(bf16[512,512]{1,0:T(8,128)(2,1)} %get-tuple-element.193), channel_id=1, source_target_pairs={{0,2},{1,3},{2,0},{3,1},{4,6},{5,7},{6,4},{7,5},{8,10},{9,11},{10,... | collective-permute-start | bytes 1572872 | tf_op jit(solution)/shard_map/ppermute | solution.py:35
Sparse Core Ops, SparseCore 0:
  132.1 92.4 reduce-scatter.2
  262.0 91.6 reduce-scatter.4
